TPU v7x, 32 devices: a whole 2x2x4 slice. The times are simulated.
32 devices in a mesh: groups: 2 (over y), gx: 8 (over z, x), gy: 2 (over core).
Axes of the slice: x: 2, y: 2, z: 4, core: 2. Of those that a mesh axis runs over, the one named last changes fastest.
Arguments:
- positions: float32 [16, 2, 3, 384], P(('groups', 'gx'), 'gy'), parts along dimension 0, may hold values from -1 to 17, as said below
- species: int32 [16, 2, 384], P(('groups', 'gx'), 'gy'), parts along dimension 0, may hold values from 0 to 4
- neighbours: int32 [16, 2, 32, 384], P(('groups', 'gx'), 'gy'), parts along dimension 0, may hold values from 0 to 1440, as said below
- send_x: int32 [16, 2, 2, 384], P(('groups', 'gx'), 'gy'), parts along dimension 0, may hold values from 0 to 383
- send_y: int32 [16, 2, 2, 144], P(('groups', 'gx'), 'gy'), parts along dimension 0, may hold values from 0 to 1151, as said below
- two_weight: float32 [18, 128], replicated, may hold values from -1.5 to 1.5
- two_bias: float32 [128], replicated, may hold values from -3 to 3
- env_weight: float32 [2, 128, 32], replicated, may hold values from -0.5 to 0.5
- value_weight: float32 [2, 128, 32], replicated, may hold values from -0.5 to 0.5
- latent_weight: float32 [2, 224, 128], replicated, may hold values from -0.375 to 0.375
- latent_bias: float32 [2, 128], replicated, may hold values from -3 to 3
- out_weight: float32 [128], replicated, may hold values from -0.5 to 0.5
- species_shift: float32 [5], replicated, may hold values from -1 to 1
Outputs:
- atom_energy: float32 [16, 2, 384], P(('groups', 'gx'), 'gy'), parts along dimension 0
- forces: float32 [16, 2, 3, 384], P(('groups', 'gx'), 'gy'), parts along dimension 0
- mean_energy: float32 [2], P('groups'), parts along dimension 0
There are 2 independent parts, one for each index of `groups`. A program takes and returns all parts, laid end to end along the dimension named above; an argument that names none is the same for every part. Nothing has to cross between parts.
Inputs may be any that keep to these rules, and one draw needn't show every extreme that they name: `neighbours`: entries equal to 1440 point to the padding slot. `send_y`: the two rows of a box hold distinct entries. `positions`: lattice sites jittered: two atoms of the extended list are at least 0.4 apart.
All inputs are finite; a program needn't handle non-finite values.
Results may differ from a plain program's by a relative error of at most 0.0003.
Values sent between devices are 32-bit elements; how exact they have to be, the bound alone decides.
No kernel may reach another device: no remote copies, remote signals or barrier semaphores. Data moves between devices by JAX's collectives and lax.ppermute only.
A program may use at most 256 MiB of HBM per device.

v0:
```python
from functools import partial
import math

import jax
import jax.numpy as jnp
from jax import lax
from jax.experimental import pallas as pl
from jax.experimental.pallas import tpu as pltpu
from jax.sharding import PartitionSpec as P

BASIS = 8
SPECIES = 5
SITES_X = 2
SITES_Y = 16
CUTOFF = 2.5
LATENT = 128
TENSORS = 32
HARM = 9
UNIT = 128
ROOT3 = math.sqrt(3.0)
DEGREE = (0, 1, 1, 1, 2, 2, 2, 2, 2)
F32 = jnp.float32
BF16 = jnp.bfloat16
WHOLE = pl.BlockSpec(memory_space=pltpu.VMEM)
SCALARS = pl.BlockSpec(memory_space=pltpu.SMEM)


def params():
    return pltpu.CompilerParams(vmem_limit_bytes=60 << 20)


def passed_along(value, axis, by):
    count = lax.axis_size(axis)
    return lax.ppermute(value, axis, [(i, (i + by) % count) for i in range(count)])


def dot(a, b):
    return jnp.dot(a, b, preferred_element_type=F32)


def dot_nt(a, b):
    return lax.dot_general(a, b, (((1,), (1,)), ((), ())), preferred_element_type=F32)


def halves(value):
    high = value.astype(BF16)
    return high, (value - high.astype(F32)).astype(BF16)


def stacked(value):
    return jnp.concatenate(halves(value), 0)


def product(weights, value):
    rows = weights.shape[0] // 2
    both = dot(weights, stacked(value))
    return both[:rows] + both[rows:]


def rounded(value):
    high = value.astype(BF16).astype(F32)
    return high, value - high


def weights_kernel(two, bias, env, val, lat, lat_bias, out_w, *outs):
    two_out, mix_out, s_out, back_out, ev_out, rad_out, cols = outs

    def depth_stack(piece):
        high, low = rounded(piece)
        top = jnp.concatenate([high, high], 0)
        bottom = jnp.concatenate([low, jnp.zeros_like(low)], 0)
        return top.T, bottom.T

    def lane_stack(piece):
        high, low = rounded(piece)
        top = jnp.concatenate([high, high], 1)
        return top, jnp.concatenate([low, jnp.zeros_like(low)], 1)

    def join(pieces):
        tops, bottoms = zip(*pieces)
        return jnp.concatenate(list(tops) + list(bottoms), 0).astype(BF16)

    def wide_stack(piece):
        return jnp.concatenate(lane_stack(piece), 0).astype(BF16)

    width = two.shape[1]
    first = jnp.concatenate(
        [
            two[0:SPECIES, :],
            bias[...],
            jnp.zeros((2, width), F32),
            two[SPECIES : 2 * SPECIES, :],
            jnp.zeros((3, width), F32),
            two[2 * SPECIES :, :],
        ],
        0,
    )
    two_out[...] = join([depth_stack(first)])
    rad_out[...] = wide_stack(two[2 * SPECIES :, :])
    for layer in range(env.shape[0]):
        latent = lat[layer]
        mix_out[layer] = join(
            [lane_stack(env[layer]), lane_stack(val[layer]), depth_stack(latent[:width])]
        )
        s_out[layer] = join([depth_stack(latent[width:])])
        back_out[layer] = wide_stack(latent)
        high = [rounded(env[layer]), rounded(val[layer])]
        top = jnp.concatenate([high[0][0], high[1][0]] * 2, 0).T
        bottom = jnp.concatenate([high[0][1], high[1][1]] + [jnp.zeros_like(high[0][1])] * 2, 0).T
        ev_out[layer] = jnp.concatenate([top, bottom], 0).astype(BF16)
    columns = jnp.concatenate(
        [lat_bias[...], out_w[...], jnp.zeros((8 - lat_bias.shape[0] - 1, width), F32)], 0
    )
    cols[...] = columns.T


def prepare_weights(two, bias, env, val, lat, lat_bias, out_w):
    layers = env.shape[0]
    shapes = [
        (2 * LATENT, 48),
        (layers, 2 * (LATENT + 2 * TENSORS), 2 * LATENT),
        (layers, 2 * LATENT, 6 * TENSORS),
        (layers, 2 * (LATENT + 3 * TENSORS), 2 * LATENT),
        (layers, 2 * LATENT, 4 * TENSORS),
        (2 * BASIS, 2 * LATENT),
    ]
    out_shape = [jax.ShapeDtypeStruct(s, BF16) for s in shapes]
    out_shape.append(jax.ShapeDtypeStruct((LATENT, 8), F32))
    return pl.pallas_call(
        weights_kernel,
        out_shape=out_shape,
        in_specs=[WHOLE] * 7,
        out_specs=[WHOLE] * 7,
        compiler_params=params(),
        name="prepare_weights",
    )(two, bias[None], env.swapaxes(1, 2), val.swapaxes(1, 2), lat, lat_bias, out_w[None])


def shifted(rows, by_x, by_y):
    lane_row = lax.broadcasted_iota(jnp.int32, rows.shape, 0)
    return rows + jnp.where(lane_row == 0, by_x, jnp.where(lane_row == 1, by_y, 0.0))


def lane_pick(table, row, index, blocks):
    low = index & 127
    high = lax.shift_right_arithmetic(index, 7)
    found = jnp.zeros(index.shape, F32)
    for block in range(blocks):
        span = slice(block * 128, block * 128 + 128)
        source = table[...][:, span] if row is None else table[row : row + 1, span]
        source = jnp.broadcast_to(source, index.shape)
        taken = jnp.take_along_axis(source, low, axis=1)
        found = jnp.where(high == block, taken, found)
    return found


def fill_wide(own, below, above, table, remap):
    atoms = own.shape[1]
    table[:, 0:atoms] = own[...]
    table[:, atoms : 2 * atoms] = shifted(below[...], -float(SITES_X), 0.0)
    table[:, 2 * atoms : 3 * atoms] = shifted(above[...], float(SITES_X), 0.0)
    lanes = lax.broadcasted_iota(jnp.int32, (1, atoms), 1).astype(F32)
    remap[:, 0:atoms] = lanes
    remap[:, atoms : 2 * atoms] = below[5:6, :] + float(atoms)
    remap[:, 2 * atoms : 3 * atoms] = above[4:5, :] + float(2 * atoms)


def lend_kernel(own, below, above, wanted, rows_out, wanted_out, table, remap):
    atoms = own.shape[1]
    blocks = 3 * atoms // 128
    fill_wide(own, below, above, table, remap)
    for tile in range(wanted.shape[1] // 128):
        span = slice(tile * 128, tile * 128 + 128)
        index = jnp.broadcast_to(wanted[:, span], (8, 128))
        place = lane_pick(remap, 0, index, blocks).astype(jnp.int32)
        place = jnp.where(index < 0, -1, place)
        wanted_out[:, span] = place[0:1]
        rows_out[:, span] = lane_pick(table, None, place, blocks)


def lend_rows(own, below, above, wanted):
    atoms = own.shape[1]
    return pl.pallas_call(
        lend_kernel,
        out_shape=[
            jax.ShapeDtypeStruct(wanted.shape[:0] + (8, wanted.shape[1]), F32),
            jax.ShapeDtypeStruct(wanted.shape, jnp.int32),
        ],
        in_specs=[WHOLE] * 4,
        out_specs=[WHOLE] * 2,
        scratch_shapes=[pltpu.VMEM((8, 3 * atoms), F32), pltpu.VMEM((1, 3 * atoms), F32)],
        compiler_params=params(),
        name="lend_rows",
    )(own, below, above, wanted)


def distances(vx, vy, vz):
    dist = jnp.sqrt(vx * vx + vy * vy + vz * vz)
    inverse = 1.0 / dist
    scaled = jnp.minimum(dist * (1.0 / CUTOFF), 1.0)
    second = scaled * scaled
    fourth = second * second
    sixth = fourth * second
    cut = 1.0 - 28.0 * sixth + 48.0 * (sixth * scaled) - 21.0 * (sixth * second)
    rest = 1.0 - scaled
    slope = (-168.0 / CUTOFF) * (fourth * scaled) * (rest * rest)
    angle = scaled * math.pi
    return inverse, cut, slope, jnp.sin(angle), jnp.cos(angle)


def geometry_kernel(
    own, below, above, across, nbrs, shift, vec_out, geo_out, nbr_out, base_out, table, remap, face
):
    atoms = own.shape[1]
    slots = nbrs.shape[0]
    blocks = table.shape[1] // 128
    fill_wide(own, below, above, table, remap)
    lanes = lax.broadcasted_iota(jnp.int32, (8, atoms), 1)
    rows = lax.broadcasted_iota(jnp.int32, (8, atoms), 0)
    moved = across[...] + jnp.where(
        rows == 1, jnp.where(lanes < face, -float(SITES_Y), float(SITES_Y)), 0.0
    )
    empty = jnp.where(rows == 2, -1000.0, jnp.where(rows == 3, -1.0, 0.0))
    table[:, 3 * atoms : 4 * atoms] = jnp.where(lanes < 2 * face, moved, empty)
    remap[:, 3 * atoms : 4 * atoms] = (
        lax.broadcasted_iota(jnp.int32, (1, atoms), 1) + 3 * atoms
    ).astype(F32)
    base = jnp.zeros((1, atoms), F32)
    for kind in range(SPECIES):
        base = base + jnp.where(own[3:4, :] == float(kind), shift[kind], 0.0)
    base_out[...] = base
    for group in range(slots // 8):
        for tile in range(atoms // UNIT):
            span = slice(tile * UNIT, tile * UNIT + UNIT)
            index = nbrs[group * 8 : group * 8 + 8, span]
            up = slice(tile * slots + group * 8, tile * slots + group * 8 + 8)
            index = lane_pick(remap, 0, index, blocks).astype(jnp.int32)
            nbr_out[up, :] = index
            vx = lane_pick(table, 0, index, blocks) - own[0:1, span]
            vy = lane_pick(table, 1, index, blocks) - own[1:2, span]
            vz = lane_pick(table, 2, index, blocks) - own[2:3, span]
            kind = lane_pick(table, 3, index, blocks)
            vec_out[0, up, :] = vx
            vec_out[1, up, :] = vy
            vec_out[2, up, :] = vz
            inverse, cut, _, sine, cosine = distances(vx, vy, vz)
            ux, uy, uz = vx * inverse, vy * inverse, vz * inverse
            harm = [
                ux,
                uy,
                uz,
                ROOT3 * ux * uy,
                ROOT3 * uy * uz,
                0.5 * (3.0 * uz * uz - 1.0),
                ROOT3 * ux * uz,
                0.5 * ROOT3 * (ux * ux - uy * uy),
            ]
            geo_out[0, up, :] = cut
            for number, value in enumerate(harm):
                geo_out[1 + number, up, :] = value
            scale = math.sqrt(2.0 / CUTOFF) * inverse * cut
            before, now = jnp.zeros_like(sine), sine
            for number in range(BASIS):
                geo_out[9 + number, up, :] = now * scale
                before, now = now, 2.0 * cosine * now - before
            geo_out[17, up, :] = kind


def geometry(own, below, above, across, nbrs, shift, face):
    slots, atoms = nbrs.shape
    return pl.pallas_call(
        partial(geometry_kernel, face=face),
        out_shape=[
            jax.ShapeDtypeStruct((3, slots * atoms // UNIT, UNIT), F32),
            jax.ShapeDtypeStruct((18, slots * atoms // UNIT, UNIT), F32),
            jax.ShapeDtypeStruct((slots * atoms // UNIT, UNIT), jnp.int32),
            jax.ShapeDtypeStruct((1, atoms), F32),
        ],
        in_specs=[WHOLE] * 5 + [SCALARS],
        out_specs=[WHOLE] * 4,
        scratch_shapes=[pltpu.VMEM((8, 4 * atoms), F32), pltpu.VMEM((1, 4 * atoms), F32)],
        compiler_params=params(),
        name="geometry",
    )(own, below, above, across, nbrs, shift)


def silu_pair(pre):
    gate = 1.0 / (1.0 + jnp.exp(-pre))
    value = pre * gate
    return value, gate + value * (1.0 - gate)


def row_spec(count, group, first):
    return pl.BlockSpec((count, group, UNIT), lambda i: (0, first + i, 0))


def index_spec(group, first):
    return pl.BlockSpec((group, UNIT), lambda i: (first + i, 0))


def edge_spec(rows, group, first):
    return pl.BlockSpec((rows, group * UNIT), lambda i: (0, first + i))


def unit_spec(rows, per):
    return pl.BlockSpec((rows, UNIT), lambda i: (0, i // per))


def edge_shape(rows, edges):
    return jax.ShapeDtypeStruct((rows, edges), F32)


def lanes_of(q):
    return slice(q * UNIT, (q + 1) * UNIT)


def rows_of(m):
    return slice(m * TENSORS, (m + 1) * TENSORS)


def add_env(geo, step, per, group, embed, env_out, norm):
    @pl.when(step % per == 0)
    def _():
        env_out[...] = jnp.zeros_like(env_out)

    cuts = [geo[0, q : q + 1, :] * norm for q in range(group)]
    for m in range(HARM):
        total = env_out[rows_of(m), :]
        for q in range(group):
            factor = cuts[q] if m == 0 else cuts[q] * geo[m, q : q + 1, :]
            total = total + embed[:TENSORS, lanes_of(q)] * factor
        env_out[rows_of(m), :] = total


def first_kernel(
    geo, own, two_w, mix_w, cols, *outs, group, per, norm
):
    x_out, slope_out, emb_out, val_out, lx_out, env_out = outs[-6:]
    step = pl.program_id(0)
    kinds = lax.broadcasted_iota(jnp.int32, (8, UNIT), 0)
    kinds_f = kinds.astype(F32)
    centre = jnp.where((own[3:4, :] == kinds_f) & (kinds < SPECIES), 1.0, 0.0)
    centre = jnp.where(kinds == SPECIES, 1.0, centre)
    parts = []
    for q in range(group):
        other = jnp.where(geo[17, q : q + 1, :] == kinds_f, 1.0, 0.0)
        radial = [geo[9 + n, q : q + 1, :] for n in range(BASIS)]
        parts.append(jnp.concatenate([centre, other] + radial, 0))
    features = jnp.concatenate(parts, 1)
    x, slope = silu_pair(product(two_w[...], features))
    x_out[...] = x
    slope_out[...] = slope
    mixed = product(mix_w[0], x)
    emb_out[...] = mixed[:TENSORS]
    val_out[...] = mixed[TENSORS : 2 * TENSORS]
    lx_out[...] = mixed[2 * TENSORS :] + cols[:, 0:1]
    add_env(geo, step, per, group, mixed, env_out, norm)


def wide_unit_spec(rows, per, first):
    return pl.BlockSpec((rows, UNIT), lambda i: (0, first + i // per))


def first_pass(geo, own, two_w, mix_w, cols, slots, group, span, before):
    edges = geo.shape[1] * UNIT
    per = slots // group
    first = span[0] * per
    rows = (LATENT, LATENT, TENSORS, TENSORS, LATENT)
    return pl.pallas_call(
        partial(first_kernel, group=group, per=per, norm=1.0 / math.sqrt(slots)),
        grid=((span[1] - span[0]) * per,),
        out_shape=[edge_shape(r, edges) for r in rows]
        + [edge_shape(HARM * TENSORS, (span[1] - span[0]) * UNIT)],
        in_specs=[row_spec(18, group, first), wide_unit_spec(8, per, span[0])]
        + [WHOLE] * 3
        + [pl.BlockSpec(memory_space=pl.ANY)] * len(before),
        out_specs=[edge_spec(r, group, first) for r in rows]
        + [unit_spec(HARM * TENSORS, per)],
        input_output_aliases={5 + n: n for n in range(len(before))},
        compiler_params=params(),
        cost_estimate=effort(64 * LATENT * LATENT * edges),
        name="first_pass",
    )(geo, own, two_w, mix_w, cols, *before)


def chosen_rows(index, columns, start):
    rows = lax.broadcasted_iota(jnp.int32, (columns, index.shape[1]), 0) + start
    return (rows == index).astype(F32).astype(BF16)


def mark_atoms(nbrs, unit, chosen):
    start = pl.multiple_of(unit * UNIT, UNIT)
    rows = lax.broadcasted_iota(jnp.int32, (UNIT, UNIT), 0)
    centre = (rows == lax.broadcasted_iota(jnp.int32, (UNIT, UNIT), 1)).astype(F32)
    for q in range(nbrs.shape[0]):
        index = nbrs[q : q + 1, :]
        chosen[:, lanes_of(q)] = chosen_rows(index, chosen.shape[0], 0)
        both = (rows + start == index).astype(F32) + centre
        chosen[pl.ds(start, UNIT), lanes_of(q)] = both.astype(BF16)


def lend_env_kernel(wanted, *refs):
    out = refs[-1]
    rows = out.shape[0]
    total = jnp.zeros((2 * rows, out.shape[1]), F32)
    start = 0
    for block in refs[:-1]:
        chosen = chosen_rows(wanted[...], block.shape[1], start)
        total = total + dot(stacked(block[...]), chosen)
        start += block.shape[1]
    out[...] = total[:rows] + total[rows:]


def lend_env(wanted, pieces):
    return pl.pallas_call(
        lend_env_kernel,
        out_shape=jax.ShapeDtypeStruct((HARM * TENSORS, wanted.shape[1]), F32),
        in_specs=[WHOLE] * (1 + len(pieces)),
        out_specs=WHOLE,
        compiler_params=params(),
        name="lend_env",
    )(wanted, *pieces)


def take_back_kernel(returned, wanted, wide, *outs, widths):
    atoms = wide.shape[1] // 3
    rows = returned.shape[0]
    value = stacked(returned[...])
    for place in range(3):
        chosen = chosen_rows(wanted[...], atoms, place * atoms)
        both = dot_nt(value, chosen)
        total = wide[:, place * atoms : (place + 1) * atoms] + both[:rows] + both[rows:]
        start = 0
        for number, width in enumerate(widths):
            outs[place * len(widths) + number][...] = total[:, start : start + width]
            start += width


def take_back(returned, wanted, wide, widths):
    outs = pl.pallas_call(
        partial(take_back_kernel, widths=widths),
        out_shape=[edge_shape(wide.shape[0], w) for w in widths] * 3,
        in_specs=[WHOLE] * 3,
        out_specs=[WHOLE] * (3 * len(widths)),
        compiler_params=params(),
        name="take_back",
    )(returned, wanted, wide)
    count = len(widths)
    return [list(outs[place * count : (place + 1) * count]) for place in range(3)]


def fill_split(pieces, split):
    rows = pieces[0].shape[0]
    start = 0
    for block in pieces:
        span = slice(start, start + block.shape[1])
        high, low = halves(block[...])
        split[:rows, span] = high
        split[rows:, span] = low
        start += block.shape[1]


def gathered(split, chosen, g):
    rows = HARM * TENSORS
    both = dot(split[...], chosen[...])
    g[...] = both[:rows] + both[rows:]


def contracted(geo, group, g, value):
    columns = []
    for q in range(group):
        span = lanes_of(q)
        sums = [g[0:TENSORS, span], None, None]
        for m in range(1, HARM):
            term = g[rows_of(m), span] * geo[m, q : q + 1, :]
            d = DEGREE[m]
            sums[d] = term if sums[d] is None else sums[d] + term
        columns.append(jnp.concatenate([part * value[:, span] for part in sums], 0))
    return jnp.concatenate(columns, 1)


def middle_kernel(*refs, group, per, norm, count, aliased, first):
    geo, nbrs, x, lx, val, s_w, mix_w, cols = refs[:8]
    pieces = refs[8 : 8 + count]
    g, slope_out, x_out, emb_out, val_out, lx_out, env_out, split, chosen = refs[
        8 + count + aliased :
    ]
    step = pl.program_id(0)

    @pl.when(step == 0)
    def _():
        fill_split(pieces, split)

    mark_atoms(nbrs, first + step // per, chosen)
    gathered(split, chosen, g)
    s = contracted(geo, group, g, val[...])
    update, slope = silu_pair(lx[...] + product(s_w[0], s))
    slope_out[...] = slope
    fresh = x[...] + update
    x_out[...] = fresh
    mixed = product(mix_w[1], fresh)
    emb_out[...] = mixed[:TENSORS]
    val_out[...] = mixed[TENSORS : 2 * TENSORS]
    lx_out[...] = mixed[2 * TENSORS :] + cols[:, 1:2]
    add_env(geo, step, per, group, mixed, env_out, norm)


def middle_pass(geo, nbrs, pieces, x, lx, val, s_w, mix_w, cols, slots, group, span, before):
    edges = x.shape[1]
    per = slots // group
    first = span[0] * per
    rows = (HARM * TENSORS, LATENT, LATENT, TENSORS, TENSORS, LATENT)
    ins = 8 + len(pieces)
    columns = sum(p.shape[1] for p in pieces)
    return pl.pallas_call(
        partial(
            middle_kernel, group=group, per=per, norm=1.0 / math.sqrt(slots),
            count=len(pieces), aliased=len(before), first=span[0],
        ),
        grid=((span[1] - span[0]) * per,),
        out_shape=[edge_shape(r, edges) for r in rows]
        + [edge_shape(HARM * TENSORS, (span[1] - span[0]) * UNIT)],
        in_specs=[row_spec(18, group, first), index_spec(group, first)]
        + [edge_spec(r, group, first) for r in (LATENT, LATENT, TENSORS)]
        + [WHOLE] * (3 + len(pieces))
        + [pl.BlockSpec(memory_space=pl.ANY)] * len(before),
        out_specs=[edge_spec(r, group, first) for r in rows]
        + [unit_spec(HARM * TENSORS, per)],
        scratch_shapes=[
            pltpu.VMEM((2 * HARM * TENSORS, columns), BF16),
            pltpu.VMEM((columns, group * UNIT), BF16),
        ],
        input_output_aliases={ins + n: n for n in range(len(before))},
        compiler_params=params(),
        cost_estimate=effort(8 * HARM * TENSORS * edges * edges // slots),
        name="middle_pass",
    )(geo, nbrs, x, lx, val, s_w, mix_w, cols, *pieces, *before)


def effort(flops):
    return pl.CostEstimate(flops=flops, transcendentals=0, bytes_accessed=flops // 512)


def pull_mixed(geo, group, g, value, ds, chosen, dgeo, wide, across, dg):
    columns = []
    for q in range(group):
        span = lanes_of(q)
        part = value[:, span]
        pulled = [ds[rows_of(d), span] for d in range(3)]
        scaled = [p * part for p in pulled]
        total = None
        for m in range(HARM):
            d = DEGREE[m]
            source = g[rows_of(m), span]
            if m == 0:
                total = source * pulled[0]
                grad = scaled[0]
            else:
                harm = geo[m, q : q + 1, :]
                total = total + source * pulled[d] * harm
                dgeo[m, q : q + 1, :] += jnp.sum(source * scaled[d], axis=0, keepdims=True)
                grad = scaled[d] * harm
            high, low = halves(grad)
            dg[rows_of(m), span] = high
            dg[rows_of(HARM + m), span] = low
        columns.append(total)
    both = dot_nt(dg[...], chosen[...])
    rows = HARM * TENSORS
    total = both[:rows] + both[rows:]
    wide[...] += total[:, : wide.shape[1]]
    across[...] += total[:, wide.shape[1] :]
    return jnp.concatenate(columns, 1)


def last_kernel(*refs, group, per, norm, count):
    geo, nbrs, x, lx, val, s_w, back_w, cols, base = refs[:9]
    pieces = refs[9 : 9 + count]
    energy, esum, dx_out, dval_out, dgeo, wide, across, split, chosen, g, dg = refs[9 + count :]
    step = pl.program_id(0)

    @pl.when(step == 0)
    def _():
        fill_split(pieces, split)
        wide[...] = jnp.zeros_like(wide)
        across[...] = jnp.zeros_like(across)
        esum[...] = jnp.zeros_like(esum)

    @pl.when(step % per == 0)
    def _():
        energy[...] = base[...]

    mark_atoms(nbrs, step // per, chosen)
    gathered(split, chosen, g)
    value = val[...]
    s = contracted(geo, group, g, value)
    update, slope = silu_pair(lx[...] + product(s_w[1], s))
    fresh = x[...] + update
    weight = cols[:, 2:3]
    read = jnp.sum(fresh * weight, axis=0, keepdims=True) * norm
    cuts = []
    dgeo[...] = jnp.zeros_like(dgeo)
    for q in range(group):
        cut = geo[0, q : q + 1, :]
        cuts.append(cut)
        energy[...] += read[:, lanes_of(q)] * cut
        dgeo[0, q : q + 1, :] = read[:, lanes_of(q)]

    @pl.when(step % per == per - 1)
    def _():
        esum[0:1, :] += energy[...]

    d_fresh = weight * (jnp.concatenate(cuts, 1) * norm)
    pulled = product(back_w[1], d_fresh * slope)
    dx_out[...] = d_fresh + pulled[:LATENT]
    dval_out[...] = pull_mixed(
        geo, group, g, value, pulled[LATENT:], chosen, dgeo, wide, across, dg
    )


def last_pass(geo, nbrs, pieces, x, lx, val, s_w, back_w, cols, base, slots, group):
    edges = x.shape[1]
    per = slots // group
    rows = HARM * TENSORS
    columns = sum(p.shape[1] for p in pieces)
    return pl.pallas_call(
        partial(
            last_kernel, group=group, per=per, norm=1.0 / math.sqrt(slots), count=len(pieces)
        ),
        grid=(geo.shape[1] // group,),
        out_shape=[
            jax.ShapeDtypeStruct(base.shape, F32),
            edge_shape(8, UNIT),
            edge_shape(LATENT, edges),
            edge_shape(TENSORS, edges),
            jax.ShapeDtypeStruct((HARM,) + geo.shape[1:], F32),
            edge_shape(rows, columns - base.shape[1]),
            edge_shape(rows, base.shape[1]),
        ],
        in_specs=[row_spec(18, group, 0), index_spec(group, 0)]
        + [edge_spec(r, group, 0) for r in (LATENT, LATENT, TENSORS)]
        + [WHOLE] * 3
        + [unit_spec(1, per)]
        + [WHOLE] * len(pieces),
        out_specs=[
            unit_spec(1, per),
            WHOLE,
            edge_spec(LATENT, group, 0),
            edge_spec(TENSORS, group, 0),
            row_spec(HARM, group, 0),
            WHOLE,
            WHOLE,
        ],
        scratch_shapes=[
            pltpu.VMEM((2 * rows, columns), BF16),
            pltpu.VMEM((columns, group * UNIT), BF16),
            pltpu.VMEM((rows, group * UNIT), F32),
            pltpu.VMEM((2 * rows, group * UNIT), BF16),
        ],
        compiler_params=params(),
        cost_estimate=effort(16 * rows * edges * edges // slots),
        name="last_pass",
    )(geo, nbrs, x, lx, val, s_w, back_w, cols, base, *pieces)


def pull_env(geo, group, total, emb, dgeo, norm):
    columns = []
    for q in range(group):
        part = emb[:, lanes_of(q)]
        cut = geo[0, q : q + 1, :] * norm
        grad = None
        for m in range(HARM):
            source = total[rows_of(m), :]
            if m == 0:
                grad = source
            else:
                grad = grad + source * geo[m, q : q + 1, :]
                dgeo[m, q : q + 1, :] += cut * jnp.sum(source * part, axis=0, keepdims=True)
        dgeo[0, q : q + 1, :] += norm * jnp.sum(grad * part, axis=0, keepdims=True)
        columns.append(grad * cut)
    return jnp.concatenate(columns, 1)


def middle_back_kernel(*refs, group, per, norm, aliased, first):
    geo, nbrs, own, low, high, dgeo_in, dx, dval, emb, g, slope, val, ev_w, back_w = refs[:14]
    wide_in, across_in = refs[14:16] if aliased else (None, None)
    dx_out, dval_out, dgeo, wide, across, total, chosen, dg = refs[14 + aliased :]
    step = pl.program_id(0)

    @pl.when(step == 0)
    def _():
        wide[...] = wide_in[...] if aliased else jnp.zeros_like(wide)
        across[...] = across_in[...] if aliased else jnp.zeros_like(across)

    @pl.when(step % per == 0)
    def _():
        total[...] = own[...] + low[...] + high[...]

    mark_atoms(nbrs, first + step // per, chosen)
    dgeo[...] = dgeo_in[...]
    demb = pull_env(geo, group, total, emb, dgeo, norm)
    d_fresh = dx[...] + product(ev_w[1], jnp.concatenate([demb, dval[...]], 0))
    pulled = product(back_w[0], d_fresh * slope[...])
    dx_out[...] = d_fresh + pulled[:LATENT]
    dval_out[...] = pull_mixed(
        geo, group, g, val[...], pulled[LATENT:], chosen, dgeo, wide, across, dg
    )


def middle_back(
    geo, nbrs, grads, dgeo, dx, dval, emb, g, slope, val, ev_w, back_w, slots, group, span, before
):
    edges = dx.shape[1]
    per = slots // group
    first = span[0] * per
    rows = HARM * TENSORS
    atoms = geo.shape[1] // slots * UNIT
    aliased = len(before)
    shapes = [
        edge_shape(LATENT, edges),
        edge_shape(TENSORS, edges),
        jax.ShapeDtypeStruct((HARM,) + geo.shape[1:], F32),
        edge_shape(rows, 3 * atoms),
        edge_shape(rows, atoms),
    ]
    extra = [*before[3:], *before[:3]]
    return pl.pallas_call(
        partial(
            middle_back_kernel, group=group, per=per, norm=1.0 / math.sqrt(slots), aliased=aliased,
            first=span[0],
        ),
        grid=((span[1] - span[0]) * per,),
        out_shape=shapes,
        in_specs=[row_spec(18, group, first), index_spec(group, first)]
        + [unit_spec(rows, per)] * 3
        + [row_spec(HARM, group, first)]
        + [
            edge_spec(r, group, first)
            for r in (LATENT, TENSORS, TENSORS, rows, LATENT, TENSORS)
        ]
        + [WHOLE] * 2
        + ([WHOLE] * 2 + [pl.BlockSpec(memory_space=pl.ANY)] * 3 if before else []),
        out_specs=[
            edge_spec(LATENT, group, first),
            edge_spec(TENSORS, group, first),
            row_spec(HARM, group, first),
            WHOLE,
            WHOLE,
        ],
        scratch_shapes=[
            pltpu.VMEM((rows, UNIT), F32),
            pltpu.VMEM((4 * atoms, group * UNIT), BF16),
            pltpu.VMEM((2 * rows, group * UNIT), BF16),
        ],
        input_output_aliases={16 + n: n for n in range(3)} if before else {},
        compiler_params=params(),
        cost_estimate=effort(8 * rows * edges * edges // slots),
        name="middle_back",
    )(geo, nbrs, *grads, dgeo, dx, dval, emb, g, slope, val, ev_w, back_w, *extra)


def first_back_kernel(
    geo, own, low, high, dgeo_in, dx, dval, emb, slope, ev_w, rad_w, *rest, group, per, norm
):
    dgeo, total = rest[-2:]
    step = pl.program_id(0)

    @pl.when(step % per == 0)
    def _():
        total[...] = own[...] + low[...] + high[...]

    dgeo[0:HARM] = dgeo_in[...]
    demb = pull_env(geo, group, total, emb, dgeo, norm)
    d_fresh = dx[...] + product(ev_w[0], jnp.concatenate([demb, dval[...]], 0))
    radial = product(rad_w[...], d_fresh * slope[...])
    for q in range(group):
        for n in range(BASIS):
            dgeo[HARM + n, q : q + 1, :] = radial[n : n + 1, lanes_of(q)]


def first_back(
    geo, grads, dgeo, dx, dval, emb, slope, ev_w, rad_w, slots, group, span, before
):
    per = slots // group
    first = span[0] * per
    rows = HARM * TENSORS
    return pl.pallas_call(
        partial(first_back_kernel, group=group, per=per, norm=1.0 / math.sqrt(slots)),
        grid=((span[1] - span[0]) * per,),
        out_shape=jax.ShapeDtypeStruct((HARM + BASIS,) + geo.shape[1:], F32),
        in_specs=[row_spec(18, group, first)]
        + [unit_spec(rows, per)] * 3
        + [row_spec(HARM, group, first)]
        + [edge_spec(r, group, first) for r in (LATENT, TENSORS, TENSORS, LATENT)]
        + [WHOLE] * 2
        + [pl.BlockSpec(memory_space=pl.ANY)] * len(before),
        out_specs=row_spec(HARM + BASIS, group, first),
        scratch_shapes=[pltpu.VMEM((rows, UNIT), F32)],
        input_output_aliases={11 + n: n for n in range(len(before))},
        compiler_params=params(),
        cost_estimate=effort(64 * LATENT * LATENT * dx.shape[1]),
        name="first_back",
    )(geo, *grads, dgeo, dx, dval, emb, slope, ev_w, rad_w, *before)


def geometry_back_kernel(vec, dgeo, nbrs, wide_out, across_out, dvec, *, slots):
    rows_total = vec.shape[1]
    units = rows_total // slots
    for group in range(rows_total // 8):
        up = slice(group * 8, group * 8 + 8)
        vx, vy, vz = (vec[axis, up, :] for axis in range(3))
        inverse, cut, slope, sine, cosine = distances(vx, vy, vz)
        ux, uy, uz = vx * inverse, vy * inverse, vz * inverse
        _, h1, h2, h3, h4, h5, h6, h7, h8 = (dgeo[m, up, :] for m in range(HARM))
        dux = h1 + ROOT3 * (uy * h4 + uz * h7 + ux * h8)
        duy = h2 + ROOT3 * (ux * h4 + uz * h5 - uy * h8)
        duz = h3 + ROOT3 * (uy * h5 + ux * h7) + 3.0 * uz * h6
        along = ux * dux + uy * duy + uz * duz
        scale = math.sqrt(2.0 / CUTOFF) * inverse
        by_wave = jnp.zeros_like(sine)
        by_angle = jnp.zeros_like(sine)
        before, now = jnp.zeros_like(sine), sine
        before_c, now_c = jnp.ones_like(sine), cosine
        for n in range(BASIS):
            pulled = dgeo[HARM + n, up, :]
            by_wave = by_wave + pulled * now
            by_angle = by_angle + (n + 1.0) * (pulled * now_c)
            before, now = now, 2.0 * cosine * now - before
            before_c, now_c = now_c, 2.0 * cosine * now_c - before_c
        d_dist = slope * dgeo[0, up, :] + scale * (
            (math.pi / CUTOFF) * by_angle * cut + by_wave * (slope - inverse * cut)
        )
        dvec[0, up, :] = (dux - ux * along) * inverse + ux * d_dist
        dvec[1, up, :] = (duy - uy * along) * inverse + uy * d_dist
        dvec[2, up, :] = (duz - uz * along) * inverse + uz * d_dist
    total = jnp.zeros((2 * 48, UNIT), F32)
    rows = lax.broadcasted_iota(jnp.int32, (16, UNIT), 0)
    lane = lax.broadcasted_iota(jnp.int32, (UNIT, UNIT), 0)
    for group in range(rows_total // 4):
        spreads, picks = [], []
        for k in range(group * 4, group * 4 + 4):
            index = nbrs[k : k + 1, :]
            here = rows == lax.shift_right_arithmetic(index, 7)
            spreads.append(
                jnp.concatenate(
                    [jnp.where(here, dvec[axis, k : k + 1, :], 0.0) for axis in range(3)], 0
                )
            )
            picks.append((lane == (index & 127)).astype(F32).astype(BF16))
        spread = jnp.concatenate(spreads, 1)
        total = total + dot_nt(stacked(spread), jnp.concatenate(picks, 1))
    total = total[:48] + total[48:]
    wide_out[...] = jnp.zeros_like(wide_out)
    across_out[...] = jnp.zeros_like(across_out)
    for axis in range(3):
        for block in range(4 * units):
            row = axis * 16 + block
            out, place = (wide_out, block) if block < 3 * units else (across_out, block - 3 * units)
            out[axis : axis + 1, lanes_of(place)] = total[row : row + 1]
        for unit in range(units):
            part = dvec[axis, unit * slots : (unit + 1) * slots, :]
            wide_out[axis : axis + 1, lanes_of(unit)] -= jnp.sum(part, axis=0, keepdims=True)


def geometry_back(vec, dgeo, nbrs, slots):
    atoms = vec.shape[1] // slots * UNIT
    return pl.pallas_call(
        partial(geometry_back_kernel, slots=slots),
        out_shape=[edge_shape(8, 3 * atoms), edge_shape(8, atoms)],
        in_specs=[WHOLE] * 3,
        out_specs=[WHOLE] * 2,
        scratch_shapes=[pltpu.VMEM(vec.shape, F32)],
        compiler_params=params(),
        name="geometry_back",
    )(vec, dgeo, nbrs)


def swap_y(rows, face):
    if lax.axis_size("gy") == 2:
        return passed_along(rows, "gy", 1)
    up = passed_along(rows[:, :face], "gy", 1)
    down = passed_along(rows[:, face:], "gy", -1)
    return jnp.concatenate([up, down], 1)


def return_y(rows, face):
    if lax.axis_size("gy") == 2:
        return passed_along(rows, "gy", 1)
    up = passed_along(rows[:, :face], "gy", -1)
    down = passed_along(rows[:, face:], "gy", 1)
    return jnp.concatenate([up, down], 1)


def ghost_rows(parts, wanted, face):
    below, above = [], []
    for part in parts:
        if below:
            part, below[-1], above[-1] = lax.optimization_barrier((part, below[-1], above[-1]))
        below.append(passed_along(part, "gx", 1))
        above.append(passed_along(part, "gx", -1))
    pieces = [*parts, *below, *above]
    return pieces + [swap_y(lend_env(wanted, pieces), face)]


def owned_grads(wide, across, wanted, face, widths, total, steps):
    across, total = lax.optimization_barrier((across, total))
    returned = return_y(across, face)
    total = sum_step(total, steps)
    own, below, above = take_back(returned, wanted, wide, widths)
    below[0], above[0], total = lax.optimization_barrier((below[0], above[0], total))
    found = []
    for number in range(len(widths)):
        send = below[number], above[number]
        if found:
            send, found[-1] = lax.optimization_barrier((send, found[-1]))
        found.append(
            [own[number], passed_along(send[0], "gx", -1), passed_along(send[1], "gx", 1)]
        )
    return found, total


def sum_steps():
    count = lax.axis_size("gx")
    if count & (count - 1) or lax.axis_size("gy") != 2:
        return None
    return [("gx", 1 << n) for n in range(count.bit_length() - 1)] + [("gy", 1)]


def sum_step(total, steps):
    if steps:
        axis, by = steps.pop(0)
        total = total + passed_along(total, axis, by)
    return total


def per_device(
    positions,
    species,
    neighbours,
    send_x,
    send_y,
    two_weight,
    two_bias,
    env_weight,
    value_weight,
    latent_weight,
    latent_bias,
    out_weight,
    species_shift,
):
    group = 16
    nbrs = neighbours[0, 0]
    atoms = nbrs.shape[1]
    face = send_y.shape[3]
    rows = jnp.concatenate(
        [
            positions[0, 0],
            species[0, 0][None].astype(F32),
            send_x[0, 0].astype(F32),
            jnp.zeros((2, atoms), F32),
        ],
        0,
    )
    wanted = jnp.concatenate(
        [
            send_y[0, 0, 1],
            send_y[0, 0, 0],
            jnp.full((atoms - 2 * face,), -1, jnp.int32),
        ]
    )[None]
    below = passed_along(rows, "gx", 1)
    above = passed_along(rows, "gx", -1)
    two_w, mix_w, s_w, back_w, ev_w, rad_w, cols = prepare_weights(
        two_weight, two_bias, env_weight, value_weight, latent_weight, latent_bias, out_weight
    )
    lent, wanted = lend_rows(rows, below, above, wanted)
    across = swap_y(lent, face)
    slots = nbrs.shape[0]
    units = atoms // UNIT
    vec, geo, nbrs, base = geometry(rows, below, above, across, nbrs, species_shift, face)
    parts, before = [], []
    for span in ((0, 1), (1, units)):
        *before, part = first_pass(
            geo, rows, two_w, mix_w, cols, slots, group, span, before
        )
        parts.append(part)
    x0, slope_a, emb0, val0, lx0 = before
    pieces = ghost_rows(parts, wanted, face)
    parts, before = [], []
    for span in ((0, units - 1), (units - 1, units)):
        *before, part = middle_pass(
            geo, nbrs, pieces, x0, lx0, val0, s_w, mix_w, cols, slots, group, span, before
        )
        parts.append(part)
    g0, slope0, x1, emb1, val1, lx1 = before
    pieces = ghost_rows(parts, wanted, face)
    energy, total, dx, dval, dgeo, wide, across = last_pass(
        geo, nbrs, pieces, x1, lx1, val1, s_w, back_w, cols, base, slots, group
    )
    steps = sum_steps()
    if steps is None:
        total = lax.psum(total, ("gx", "gy"))
    grads, total = owned_grads(wide, across, wanted, face, (UNIT, atoms - UNIT), total, steps)
    before = []
    for number, span in enumerate(((0, 1), (1, units))):
        before = middle_back(
            geo, nbrs, grads[number], dgeo, dx, dval, emb1, g0, slope0, val0, ev_w, back_w,
            slots, group, span, before,
        )
    dx, dval, dgeo, wide, across = before
    grads, total = owned_grads(wide, across, wanted, face, (atoms - UNIT, UNIT), total, steps)
    before = []
    for number, span in enumerate(((0, units - 1), (units - 1, units))):
        before = [
            first_back(
                geo, grads[number], dgeo, dx, dval, emb0, slope_a, ev_w, rad_w, slots, group,
                span, before,
            )
        ]
    wide, across = geometry_back(vec, before[0], nbrs, slots)
    grads, total = owned_grads(wide, across, wanted, face, (atoms,), total, steps)
    while steps:
        total = sum_step(total, steps)
    mean_energy = jnp.sum(total) / (atoms * lax.axis_size("gx") * lax.axis_size("gy"))
    forces = -(grads[0][0] + grads[0][1] + grads[0][2])[:3]
    return (energy[None], forces[None, None], mean_energy.reshape(1))


def solution(mesh):
    placed = (
        P(("groups", "gx"), "gy", None, None),
        P(("groups", "gx"), "gy", None),
        P(("groups", "gx"), "gy", None, None),
        P(("groups", "gx"), "gy", None, None),
        P(("groups", "gx"), "gy", None, None),
        P(),
        P(),
        P(),
        P(),
        P(),
        P(),
        P(),
        P(),
    )
    return jax.shard_map(
        per_device,
        mesh=mesh,
        in_specs=placed,
        out_specs=(
            P(("groups", "gx"), "gy", None),
            P(("groups", "gx"), "gy", None, None),
            P("groups"),
        ),
        check_vma=False,
    )
```

profile of v0, /device:TPU:0, one launch (start us, length us, event | category | flops | bytes accessed | tf_op | source)
XLA Modules:
  0.0 384.4 jit_solution(14616847044020839740)
XLA Ops:
  2.8 6.0 %collective-permute-start.1 = (f32[8,384]{1,0:T(8,128)S(1)}, f32[8,384]{1,0:T(8,128)S(1)}, u32[]{:S(2)}, u32[]{:S(2)}) collective-permute-start(f32[8,384]{1,0:T(8,128)S(1)} %maximum_maximum_fusion.own), channel_id=1, source_target_pairs={{0,14},{2,0},{4,2},{6,4},{8,6},{10,8},{12,10},{14,12},{1,15},{3,1}... | collective-permute-start | bytes 36872 | tf_op jit(solution)/shard_map/ppermute | solution.py:34
  10.2 5.0 %collective-permute-done.below = f32[8,384]{1,0:T(8,128)S(1)} collective-permute-done((f32[8,384]{1,0:T(8,128)S(1)}, f32[8,384]{1,0:T(8,128)S(1)}, u32[]{:S(2)}, u32[]{:S(2)}) %collective-permute-start) | collective-permute-done | bytes 12320 | tf_op jit(solution)/shard_map/ppermute | solution.py:34
  17.4 2.2 prepare_weights.1
  20.2 3.5 geometry.1
  23.7 5.3 %first_pass.2 = (f32[128,12288]{1,0:T(8,128)}, f32[128,12288]{1,0:T(8,128)}, f32[32,12288]{1,0:T(8,128)}, f32[32,12288]{1,0:T(8,128)}, f32[128,12288]{1,0:T(8,128)}, /*index=5*/f32[288,128]{1,0:T(8,128)}) custom-call(f32[18,96,128]{2,1,0:T(8,128)} %get-tuple-element.108.geo.refs_0_, f32[8,384]{1,0:T(8,128)} %copy-done.13, ...), custom_call_target="tpu_custom_call" | custom-call | flops 12884901888 | bytes 25165824 | tf_op jit(solution)/shard_map/first_pass/pallas_call | solution.py:369
  31.0 8.1 %first_pass.3 = (f32[128,12288]{1,0:T(8,128)}, f32[128,12288]{1,0:T(8,128)}, f32[32,12288]{1,0:T(8,128)}, f32[32,12288]{1,0:T(8,128)}, f32[128,12288]{1,0:T(8,128)}, /*index=5*/f32[288,256]{1,0:T(8,128)}) custom-call(f32[18,96,128]{2,1,0:T(8,128)} %get-tuple-element.108.geo.refs_0_, ...), custom_call_target="tpu_custom_call", output_to_operand_aliasing={{0}: (5, {}), {1}: (6, {}), {2}: (7, {}), {3}: (8, {}), {4}... | custom-call | flops 12884901888 | bytes 25165824 | tf_op jit(solution)/shard_map/first_pass/pallas_call | solution.py:369
  39.2 3.3 collective-permute-start.6
  42.8 11.8 %collective-permute-done.6.refs_5_.refs_13_ = f32[288,256]{1,0:T(8,128)S(1)} collective-permute-done((f32[288,256]{1,0:T(8,128)}, f32[288,256]{1,0:T(8,128)S(1)}, u32[]{:S(2)}, u32[]{:S(2)}) %collective-permute-start.6) | collective-permute-done | bytes 294944 | tf_op jit(solution)/shard_map/ppermute | solution.py:34
  55.4 3.1 lend_env.2
  61.3 41.1 %middle_pass.2 = (f32[288,12288]{1,0:T(8,128)}, f32[128,12288]{1,0:T(8,128)}, f32[128,12288]{1,0:T(8,128)}, f32[32,12288]{1,0:T(8,128)}, f32[32,12288]{1,0:T(8,1...) custom-call(f32[18,96,128]{2,1,0:T(8,128)} %get-tuple-element.108.geo.refs_0_, s32[96,128]{1,0:T(8,128)} %get-tuple-element.109.refs_1_.nbrs, ...), custom_call_target="tpu_custom_call" | custom-call | flops 10871635968 | bytes 21233664 | tf_op jit(solution)/shard_map/middle_pass/pallas_call | solution.py:515
  102.4 3.6 collective-permute-start.9
  106.6 23.1 %middle_pass.3 = (f32[288,12288]{1,0:T(8,128)}, f32[128,12288]{1,0:T(8,128)}, f32[128,12288]{1,0:T(8,128)}, f32[32,12288]{1,0:T(8,128)}, f32[32,12288]{1,0:T(8,1...) custom-call(f32[18,96,128]{2,1,0:T(8,128)} %get-tuple-element.108.ge, ...), custom_call_target="tpu_custom_call", output_to_operand_aliasing={{0}: (15, {}), {1}: (16, {}), {2}: (17, {}), {3}: (18, {}),... | custom-call | flops 10871635968 | bytes 21233664 | tf_op jit(solution)/shard_map/middle_pass/pallas_call | solution.py:515
  129.7 4.7 %collective-permute-start.11 = (f32[288,128]{1,0:T(8,128)}, f32[288,128]{1,0:T(8,128)S(1)}, u32[]{:S(2)}, u32[]{:S(2)}) collective-permute-start(f32[288,128]{1,0:T(8,128)} %get-tuple-element.142.refs_1_.refs_10_), channel_id=1, source_target_pairs={{0,14},{2,0},{4,2},{6,4},{8,6},{10,8},{12,10},{14,12},{1,15},{3,1}... | collective-permute-start | bytes 442376 | tf_op jit(solution)/shard_map/ppermute | solution.py:34
  134.6 3.0 collective-permute-done.11.refs_5_.refs_14_
  137.6 5.0 %collective-permute-done.10.refs_3_.refs_12_ = f32[288,128]{1,0:T(8,128)S(1)} collective-permute-done((f32[288,128]{1,0:T(8,128)}, f32[288,128]{1,0:T(8,128)S(1)}, u32[]{:S(2)}, u32[]{:S(2)}) %collective-permute-start.10) | collective-permute-done | bytes 147488 | tf_op jit(solution)/shard_map/ppermute | solution.py:34
  143.3 3.0 lend_env.3
  149.1 82.5 %last_pass.1 = (f32[1,384]{1,0:T(1,128)}, f32[8,128]{1,0:T(8,128)}, f32[128,12288]{1,0:T(8,128)}, f32[32,12288]{1,0:T(8,128)}, f32[9,96,128]{2,1,0:T(8,128)}, /*index=5*/f32[288,1152]{1,0:T(8,128)}, f32[288,384]{1,0:T(8,128)}) custom-call(f32[18,96,128]{2,1,0:T(8,128)} %get-tuple-element.108.geo.refs_0_, s32[96,128]{1,0:T(8,128)} %get-tuple-element.109.refs_1_.nbrs, ...), custom_call_target="tpu_custom_call" | custom-call | flops 21743271936 | bytes 42467328 | tf_op jit(solution)/shard_map/last_pass/pallas_call | solution.py:625
  232.1 6.5 %collective-permute-done.14 = f32[8,128]{1,0:T(8,128)S(1)} collective-permute-done((f32[8,128]{1,0:T(8,128)}, f32[8,128]{1,0:T(8,128)S(1)}, u32[]{:S(2)}, u32[]{:S(2)}) %collective-permute-start.14) | collective-permute-done | bytes 4128 | tf_op jit(solution)/shard_map/ppermute | solution.py:34
  240.1 3.2 take_back.3
  243.3 2.0 collective-permute-start.16
  245.3 6.5 %collective-permute-done.15.refs_3_ = f32[288,128]{1,0:T(8,128)S(1)} collective-permute-done((f32[288,128]{1,0:T(8,128)}, f32[288,128]{1,0:T(8,128)S(1)}, u32[]{:S(2)}, u32[]{:S(2)}) %collective-permute-start.15) | collective-permute-done | bytes 147488 | tf_op jit(solution)/shard_map/ppermute | solution.py:34
  253.9 23.1 %middle_back.2 = (f32[128,12288]{1,0:T(8,128)}, f32[32,12288]{1,0:T(8,128)}, f32[9,96,128]{2,1,0:T(8,128)}, f32[288,1152]{1,0:T(8,128)}, f32[288,384]{1,0:T(8,128)}) custom-call(f32[18,96,128]{2,1,0:T(8,128)} %get-tuple-element.108.geo.refs_0_, s32[96,128]{1,0:T(8,128)} %get-tuple-element.109.refs_1_.nbrs, f32[288,128]{1,0:T(8,128)} %get-tuple-element.168.refs_2_, ...), custom_call_target="tpu_custom_call" | custom-call | flops 10871635968 | bytes 21233664 | tf_op jit(solution)/shard_map/middle_back/pallas_call | solution.py:726
  277.8 42.8 %middle_back.3 = (f32[128,12288]{1,0:T(8,128)}, f32[32,12288]{1,0:T(8,128)}, f32[9,96,128]{2,1,0:T(8,128)}, f32[288,1152]{1,0:T(8,128)}, f32[288,384]{1,0:T(8,128)}) custom-call(f32[18,96,128]{2,1,0:T(8,128)} %get-tuple-element.108.geo.refs_0_, ...), custom_call_target="tpu_custom_call", output_to_operand_aliasing={{0}: (16, {}), {1}: (17, {}), {2}: (18, {})} | custom-call | flops 10871635968 | bytes 21233664 | tf_op jit(solution)/shard_map/middle_back/pallas_call | solution.py:726
  320.8 5.4 %collective-permute-done.20 = f32[8,128]{1,0:T(8,128)S(1)} collective-permute-done((f32[8,128]{1,0:T(8,128)S(1)}, f32[8,128]{1,0:T(8,128)S(1)}, u32[]{:S(2)}, u32[]{:S(2)}) %collective-permute-start.20) | collective-permute-done | bytes 4128 | tf_op jit(solution)/shard_map/ppermute | solution.py:34
  327.0 3.3 take_back.4
  332.2 12.7 %collective-permute-done.21.low = f32[288,256]{1,0:T(8,128)S(1)} collective-permute-done((f32[288,256]{1,0:T(8,128)}, f32[288,256]{1,0:T(8,128)S(1)}, u32[]{:S(2)}, u32[]{:S(2)}) %collective-permute-start.21) | collective-permute-done | bytes 294944 | tf_op jit(solution)/shard_map/ppermute | solution.py:34
  347.0 8.2 %first_back.2.rest_0_ = f32[17,96,128]{2,1,0:T(8,128)} custom-call(f32[18,96,128]{2,1,0:T(8,128)} %get-tuple-element.108.geo.refs_0_, f32[288,256]{1,0:T(8,128)} %get-tuple-element.197.own, f32[288,256]{1,0:T(8,128)} %copy-done.19, f32[288,256]{1,0:T(8,128)} %copy-done.20, f32[9,96,128]{2,1,0:T(8,128)} %get-tuple-element.191.dgeo_in, ...), custom_call_target="tpu_custom_call" | custom-call | flops 12884901888 | bytes 25165824 | tf_op jit(solution)/shard_map/first_back/pallas_call | solution.py:786
  356.0 4.7 %first_back.3.dgeo = f32[17,96,128]{2,1,0:T(8,128)} custom-call(f32[18,96,128]{2,1,0:T(8,128)} %get-tuple-element.108.geo.refs_0_, f32[288,128]{1,0:T(8,128)} %get-tuple-element.180.own, f32[288,128]{1,0:T(8,128)} %copy-done.21, f32[288,128]{1,0:T(8,128)} %copy-done.23, f32[9,96,128]{2,1,0:T(8,128)} %get-tuple-element.191.dgeo_in, ...), custom_call_target="tpu_custom_call", output_to_operand_aliasing={{}: (11, {})} | custom-call | flops 12884901888 | bytes 25165824 | tf_op jit(solution)/shard_map/first_back/pallas_call | solution.py:786
  360.7 3.4 geometry_back.1
  364.1 4.5 %collective-permute-done.26 = f32[8,128]{1,0:T(8,128)S(1)} collective-permute-done((f32[8,128]{1,0:T(8,128)S(1)}, f32[8,128]{1,0:T(8,128)S(1)}, u32[]{:S(2)}, u32[]{:S(2)}) %collective-permute-start.26) | collective-permute-done | bytes 4128 | tf_op jit(solution)/shard_map/ppermute | solution.py:34
  371.0 3.9 %collective-permute-start.27 = (f32[8,384]{1,0:T(8,128)}, f32[8,384]{1,0:T(8,128)S(1)}, u32[]{:S(2)}, u32[]{:S(2)}) collective-permute-start(f32[8,384]{1,0:T(8,128)} %get-tuple-element.208), channel_id=1, source_target_pairs={{0,14},{2,0},{4,2},{6,4},{8,6},{10,8},{12,10},{14,12},{1,15},{3,1}... | collective-permute-start | bytes 36872 | tf_op jit(solution)/shard_map/ppermute | solution.py:34
  376.5 5.0 %collective-permute-done.28 = f32[8,384]{1,0:T(8,128)S(1)} collective-permute-done((f32[8,384]{1,0:T(8,128)}, f32[8,384]{1,0:T(8,128)S(1)}, u32[]{:S(2)}, u32[]{:S(2)}) %collective-permute-start.28) | collective-permute-done | bytes 12320 | tf_op jit(solution)/shard_map/ppermute | solution.py:34
  (112 shorter events, 31.7 us)
Async XLA Ops:
  2.8 7.4 %collective-permute-start.1 = (f32[8,384]{1,0:T(8,128)S(1)}, f32[8,384]{1,0:T(8,128)S(1)}, u32[]{:S(2)}, u32[]{:S(2)}) collective-permute-start(f32[8,384]{1,0:T(8,128)S(1)} %maximum_maximum_fusion.own), channel_id=1, source_target_pairs={{0,14},{2,0},{4,2},{6,4},{8,6},{10,8},{12,10},{14,12},{1,15},{3,1}... | collective-permute-start | bytes 36872 | tf_op jit(solution)/shard_map/ppermute | solution.py:34
  8.8 6.4 %collective-permute-start = (f32[8,384]{1,0:T(8,128)S(1)}, f32[8,384]{1,0:T(8,128)S(1)}, u32[]{:S(2)}, u32[]{:S(2)}) collective-permute-start(f32[8,384]{1,0:T(8,128)S(1)} %maximum_maximum_fusion.own), channel_id=1, source_target_pairs={{0,2},{2,4},{4,6},{6,8},{8,10},{10,12},{12,14},{14,0},{1,3},{3,5},... | collective-permute-start | bytes 36872 | tf_op jit(solution)/shard_map/ppermute | solution.py:34
  17.4 2.2 collective-permute-start.2
  29.0 10.2 %collective-permute-start.4 = (f32[288,128]{1,0:T(8,128)}, f32[288,128]{1,0:T(8,128)S(1)}, u32[]{:S(2)}, u32[]{:S(2)}) collective-permute-start(f32[288,128]{1,0:T(8,128)} %get-tuple-element.122.refs_0_.refs_8_), channel_id=1, source_target_pairs={{0,14},{2,0},{4,2},{6,4},{8,6},{10,8},{12,10},{14,12},{1,15},{3,1}... | collective-permute-start | bytes 442376 | tf_op jit(solution)/shard_map/ppermute | solution.py:34
  29.6 9.6 %collective-permute-start.3 = (f32[288,128]{1,0:T(8,128)}, f32[288,128]{1,0:T(8,128)S(1)}, u32[]{:S(2)}, u32[]{:S(2)}) collective-permute-start(f32[288,128]{1,0:T(8,128)} %get-tuple-element.122.refs_0_.refs_8_), channel_id=1, source_target_pairs={{0,2},{2,4},{4,6},{6,8},{8,10},{10,12},{12,14},{14,0},{1,3},{3,5},... | collective-permute-start | bytes 442376 | tf_op jit(solution)/shard_map/ppermute | solution.py:34
  39.1 15.5 %copy-start.2 = (f32[288,128]{1,0:T(8,128)}, f32[288,128]{1,0:T(8,128)S(1)}, u32[]{:S(2)}) copy-start(f32[288,128]{1,0:T(8,128)S(1)} %collective-permute-done.4.refs_4_.refs_12_) | copy-start | bytes 442372
  39.1 15.4 %copy-start.3 = (f32[288,128]{1,0:T(8,128)}, f32[288,128]{1,0:T(8,128)S(1)}, u32[]{:S(2)}) copy-start(f32[288,128]{1,0:T(8,128)S(1)} %collective-permute-done.3.refs_2_.refs_10_) | copy-start | bytes 442372
  39.2 15.4 %collective-permute-start.6 = (f32[288,256]{1,0:T(8,128)}, f32[288,256]{1,0:T(8,128)S(1)}, u32[]{:S(2)}, u32[]{:S(2)}) collective-permute-start(f32[288,256]{1,0:T(8,128)} %get-tuple-element.125.refs_1_.refs_9_), channel_id=1, source_target_pairs={{0,14},{2,0},{4,2},{6,4},{8,6},{10,8},{12,10},{14,12},{1,15},{3,1}... | collective-permute-start | bytes 884744 | tf_op jit(solution)/shard_map/ppermute | solution.py:34
  42.5 12.1 %collective-permute-start.5 = (f32[288,256]{1,0:T(8,128)}, f32[288,256]{1,0:T(8,128)S(1)}, u32[]{:S(2)}, u32[]{:S(2)}) collective-permute-start(f32[288,256]{1,0:T(8,128)} %get-tuple-element.125.refs_1_.refs_9_), channel_id=1, source_target_pairs={{0,2},{2,4},{4,6},{6,8},{8,10},{10,12},{12,14},{14,0},{1,3},{3,5},... | collective-permute-start | bytes 884744 | tf_op jit(solution)/shard_map/ppermute | solution.py:34
  58.5 2.0 collective-permute-start.7
  102.4 27.3 %collective-permute-start.9 = (f32[288,256]{1,0:T(8,128)}, f32[288,256]{1,0:T(8,128)S(1)}, u32[]{:S(2)}, u32[]{:S(2)}) collective-permute-start(f32[288,256]{1,0:T(8,128)} %get-tuple-element.139.refs_0_.refs_9_), channel_id=1, source_target_pairs={{0,14},{2,0},{4,2},{6,4},{8,6},{10,8},{12,10},{14,12},{1,15},{3,1}... | collective-permute-start | bytes 884744 | tf_op jit(solution)/shard_map/ppermute | solution.py:34
  106.0 23.7 %collective-permute-start.8 = (f32[288,256]{1,0:T(8,128)}, f32[288,256]{1,0:T(8,128)S(1)}, u32[]{:S(2)}, u32[]{:S(2)}) collective-permute-start(f32[288,256]{1,0:T(8,128)} %get-tuple-element.139.refs_0_.refs_9_), channel_id=1, source_target_pairs={{0,2},{2,4},{4,6},{6,8},{8,10},{10,12},{12,14},{14,0},{1,3},{3,5},... | collective-permute-start | bytes 884744 | tf_op jit(solution)/shard_map/ppermute | solution.py:34
  129.7 7.9 %collective-permute-start.11 = (f32[288,128]{1,0:T(8,128)}, f32[288,128]{1,0:T(8,128)S(1)}, u32[]{:S(2)}, u32[]{:S(2)}) collective-permute-start(f32[288,128]{1,0:T(8,128)} %get-tuple-element.142.refs_1_.refs_10_), channel_id=1, source_target_pairs={{0,14},{2,0},{4,2},{6,4},{8,6},{10,8},{12,10},{14,12},{1,15},{3,1}... | collective-permute-start | bytes 442376 | tf_op jit(solution)/shard_map/ppermute | solution.py:34
  134.5 8.2 %collective-permute-start.10 = (f32[288,128]{1,0:T(8,128)}, f32[288,128]{1,0:T(8,128)S(1)}, u32[]{:S(2)}, u32[]{:S(2)}) collective-permute-start(f32[288,128]{1,0:T(8,128)} %get-tuple-element.142.refs_1_.refs_10_), channel_id=1, source_target_pairs={{0,2},{2,4},{4,6},{6,8},{8,10},{10,12},{12,14},{14,0},{1,3},{3,5},... | collective-permute-start | bytes 442376 | tf_op jit(solution)/shard_map/ppermute | solution.py:34
  146.4 2.0 collective-permute-start.12
  231.7 7.6 %collective-permute-start.13 = (f32[288,384]{1,0:T(8,128)}, f32[288,384]{1,0:T(8,128)S(1)}, u32[]{:S(2)}, u32[]{:S(2)}) collective-permute-start(f32[288,384]{1,0:T(8,128)} %get-tuple-element.148), channel_id=1, source_target_pairs={{0,1},{1,0},{2,3},{3,2},{4,5},{5,4},{6,7},{7,6},{8,9},{9,8},{10,11... | collective-permute-start | bytes 1327112 | tf_op jit(solution)/shard_map/ppermute | solution.py:34
  231.9 6.7 %collective-permute-start.14 = (f32[8,128]{1,0:T(8,128)}, f32[8,128]{1,0:T(8,128)S(1)}, u32[]{:S(2)}, u32[]{:S(2)}) collective-permute-start(f32[8,128]{1,0:T(8,128)} %get-tuple-element.156), channel_id=1, source_target_pairs={{0,2},{2,4},{4,6},{6,8},{8,10},{10,12},{12,14},{14,0},{1,3},{3,5},... | collective-permute-start | bytes 12296 | tf_op jit(solution)/shard_map/ppermute | solution.py:34
  243.3 8.5 %collective-permute-start.15 = (f32[288,128]{1,0:T(8,128)}, f32[288,128]{1,0:T(8,128)S(1)}, u32[]{:S(2)}, u32[]{:S(2)}) collective-permute-start(f32[288,128]{1,0:T(8,128)} %get-tuple-element.157), channel_id=1, source_target_pairs={{0,14},{2,0},{4,2},{6,4},{8,6},{10,8},{12,10},{14,12},{1,15},{3,1}... | collective-permute-start | bytes 442376 | tf_op jit(solution)/shard_map/ppermute | solution.py:34
  243.3 8.5 %collective-permute-start.16 = (f32[288,128]{1,0:T(8,128)}, f32[288,128]{1,0:T(8,128)S(1)}, u32[]{:S(2)}, u32[]{:S(2)}) collective-permute-start(f32[288,128]{1,0:T(8,128)} %get-tuple-element.158), channel_id=1, source_target_pairs={{0,2},{2,4},{4,6},{6,8},{8,10},{10,12},{12,14},{14,0},{1,3},{3,5},... | collective-permute-start | bytes 442376 | tf_op jit(solution)/shard_map/ppermute | solution.py:34
  251.8 25.2 %collective-permute-start.17 = (f32[288,256]{1,0:T(8,128)}, f32[288,256]{1,0:T(8,128)S(1)}, u32[]{:S(2)}, u32[]{:S(2)}) collective-permute-start(f32[288,256]{1,0:T(8,128)} %get-tuple-element.159), channel_id=1, source_target_pairs={{0,14},{2,0},{4,2},{6,4},{8,6},{10,8},{12,10},{14,12},{1,15},{3,1}... | collective-permute-start | bytes 884744 | tf_op jit(solution)/shard_map/ppermute | solution.py:34
  251.9 25.1 %collective-permute-start.18 = (f32[288,256]{1,0:T(8,128)}, f32[288,256]{1,0:T(8,128)S(1)}, u32[]{:S(2)}, u32[]{:S(2)}) collective-permute-start(f32[288,256]{1,0:T(8,128)} %get-tuple-element.160), channel_id=1, source_target_pairs={{0,2},{2,4},{4,6},{6,8},{8,10},{10,12},{12,14},{14,0},{1,3},{3,5},... | collective-permute-start | bytes 884744 | tf_op jit(solution)/shard_map/ppermute | solution.py:34
  320.6 5.5 %collective-permute-start.19 = (f32[288,384]{1,0:T(8,128)}, f32[288,384]{1,0:T(8,128)S(1)}, u32[]{:S(2)}, u32[]{:S(2)}) collective-permute-start(f32[288,384]{1,0:T(8,128)} %get-tuple-element.178), channel_id=1, source_target_pairs={{0,1},{1,0},{2,3},{3,2},{4,5},{5,4},{6,7},{7,6},{8,9},{9,8},{10,11... | collective-permute-start | bytes 1327112 | tf_op jit(solution)/shard_map/ppermute | solution.py:34
  320.7 5.5 %collective-permute-start.20 = (f32[8,128]{1,0:T(8,128)S(1)}, f32[8,128]{1,0:T(8,128)S(1)}, u32[]{:S(2)}, u32[]{:S(2)}) collective-permute-start(f32[8,128]{1,0:T(8,128)S(1)} %add.18), channel_id=1, source_target_pairs={{0,4},{2,6},{4,8},{6,10},{8,12},{10,14},{12,0},{14,2},{1,5},{3,7},... | collective-permute-start | bytes 12296 | tf_op jit(solution)/shard_map/ppermute | solution.py:34
  330.2 14.7 %collective-permute-start.21 = (f32[288,256]{1,0:T(8,128)}, f32[288,256]{1,0:T(8,128)S(1)}, u32[]{:S(2)}, u32[]{:S(2)}) collective-permute-start(f32[288,256]{1,0:T(8,128)} %get-tuple-element.187), channel_id=1, source_target_pairs={{0,14},{2,0},{4,2},{6,4},{8,6},{10,8},{12,10},{14,12},{1,15},{3,1}... | collective-permute-start | bytes 884744 | tf_op jit(solution)/shard_map/ppermute | solution.py:34
  331.2 13.8 %collective-permute-start.22 = (f32[288,256]{1,0:T(8,128)}, f32[288,256]{1,0:T(8,128)S(1)}, u32[]{:S(2)}, u32[]{:S(2)}) collective-permute-start(f32[288,256]{1,0:T(8,128)} %get-tuple-element.188), channel_id=1, source_target_pairs={{0,2},{2,4},{4,6},{6,8},{8,10},{10,12},{12,14},{14,0},{1,3},{3,5},... | collective-permute-start | bytes 884744 | tf_op jit(solution)/shard_map/ppermute | solution.py:34
  345.0 10.3 %collective-permute-start.23 = (f32[288,128]{1,0:T(8,128)}, f32[288,128]{1,0:T(8,128)S(1)}, u32[]{:S(2)}, u32[]{:S(2)}) collective-permute-start(f32[288,128]{1,0:T(8,128)} %get-tuple-element.189), channel_id=1, source_target_pairs={{0,14},{2,0},{4,2},{6,4},{8,6},{10,8},{12,10},{14,12},{1,15},{3,1}... | collective-permute-start | bytes 442376 | tf_op jit(solution)/shard_map/ppermute | solution.py:34
  346.2 9.1 %collective-permute-start.24 = (f32[288,128]{1,0:T(8,128)}, f32[288,128]{1,0:T(8,128)S(1)}, u32[]{:S(2)}, u32[]{:S(2)}) collective-permute-start(f32[288,128]{1,0:T(8,128)} %get-tuple-element.190), channel_id=1, source_target_pairs={{0,2},{2,4},{4,6},{6,8},{8,10},{10,12},{12,14},{14,0},{1,3},{3,5},... | collective-permute-start | bytes 442376 | tf_op jit(solution)/shard_map/ppermute | solution.py:34
  364.1 4.5 %collective-permute-start.25 = (f32[8,384]{1,0:T(8,128)}, f32[8,384]{1,0:T(8,128)S(1)}, u32[]{:S(2)}, u32[]{:S(2)}) collective-permute-start(f32[8,384]{1,0:T(8,128)} %get-tuple-element.202), channel_id=1, source_target_pairs={{0,1},{1,0},{2,3},{3,2},{4,5},{5,4},{6,7},{7,6},{8,9},{9,8},{10,11... | collective-permute-start | bytes 36872 | tf_op jit(solution)/shard_map/ppermute | solution.py:34
  364.1 4.5 %collective-permute-start.26 = (f32[8,128]{1,0:T(8,128)S(1)}, f32[8,128]{1,0:T(8,128)S(1)}, u32[]{:S(2)}, u32[]{:S(2)}) collective-permute-start(f32[8,128]{1,0:T(8,128)S(1)} %add.19), channel_id=1, source_target_pairs={{0,8},{2,10},{4,12},{6,14},{8,0},{10,2},{12,4},{14,6},{1,9},{3,11}... | collective-permute-start | bytes 12296 | tf_op jit(solution)/shard_map/ppermute | solution.py:34
  371.0 3.9 %collective-permute-start.29 = (f32[8,128]{1,0:T(8,128)S(1)}, f32[8,128]{1,0:T(8,128)S(1)}, u32[]{:S(2)}, u32[]{:S(2)}) collective-permute-start(f32[8,128]{1,0:T(8,128)S(1)} %add.20), channel_id=1, source_target_pairs={{0,1},{1,0},{2,3},{3,2},{4,5},{5,4},{6,7},{7,6},{8,9},{9,8},{10,11... | collective-permute-start | bytes 12296 | tf_op jit(solution)/shard_map/ppermute | solution.py:34
  371.0 5.5 %collective-permute-start.27 = (f32[8,384]{1,0:T(8,128)}, f32[8,384]{1,0:T(8,128)S(1)}, u32[]{:S(2)}, u32[]{:S(2)}) collective-permute-start(f32[8,384]{1,0:T(8,128)} %get-tuple-element.208), channel_id=1, source_target_pairs={{0,14},{2,0},{4,2},{6,4},{8,6},{10,8},{12,10},{14,12},{1,15},{3,1}... | collective-permute-start | bytes 36872 | tf_op jit(solution)/shard_map/ppermute | solution.py:34
  374.9 6.6 %collective-permute-start.28 = (f32[8,384]{1,0:T(8,128)}, f32[8,384]{1,0:T(8,128)S(1)}, u32[]{:S(2)}, u32[]{:S(2)}) collective-permute-start(f32[8,384]{1,0:T(8,128)} %get-tuple-element.209), channel_id=1, source_target_pairs={{0,2},{2,4},{4,6},{6,8},{8,10},{10,12},{12,14},{14,0},{1,3},{3,5},... | collective-permute-start | bytes 36872 | tf_op jit(solution)/shard_map/ppermute | solution.py:34
  (23 other events, 66.7 us)
where the time goes:
time: 389 us; the launch traced here: 384 us
  Pallas kernels  264 us (68%)
  waiting for transfers between devices  69.8 us (18%)
  starting transfers between devices  33.4 us (9%)
  local copies, waits for them, and re-layouts  10.6 us (3%)
    pallas_call x1, Pallas kernels, last_pass(): pl.pallas_call(partial(last_kernel, group=group, per=per, norm=1.0 / math...  82.5 us
    ppermute x30, waiting for transfers between devices, passed_along(): lax.ppermute(value, axis, [(i, (i + by) % count) for i in range(count)])  69.8 us
    pallas_call x2, Pallas kernels, middle_back(): pl.pallas_call(partial(middle_back_kernel, group=group, per=per, norm=1.0...  65.9 us
    pallas_call x2, Pallas kernels, middle_pass(): pl.pallas_call(partial(middle_kernel, group=group, per=per, norm=1.0 / ma...  64.2 us
    ppermute x30, starting transfers between devices, passed_along(): lax.ppermute(value, axis, [(i, (i + by) % count) for i in range(count)])  33.4 us
    pallas_call x2, Pallas kernels, first_pass(): pl.pallas_call(partial(first_kernel, group=group, per=per, norm=1.0 / mat...  13.4 us
    pallas_call x2, Pallas kernels, first_back(): pl.pallas_call(partial(first_back_kernel, group=group, per=per, norm=1.0...  12.9 us
    unnamed x52, local copies, waits for them, and re-layouts  9.19 us
  transfers between devices with their start and end apart: 30, of which 13 were waited for; matrix products, arithmetic and copies ran while one was open for 1% of the time, Pallas kernels for 17%

commit v1 on v0

--- a/solution.py
+++ b/solution.py
@@ -176,6 +176,29 @@
         place = jnp.where(index < 0, -1, place)
         wanted_out[:, span] = place[0:1]
         rows_out[:, span] = lane_pick(table, None, place, blocks)
+
+
+def pack_kernel(coords, species, lend_x, lend_y, rows, wanted):
+    face = lend_y.shape[1]
+    rows[...] = jnp.zeros_like(rows)
+    rows[0:3, :] = coords[...]
+    rows[3:4, :] = species[...].astype(F32)
+    rows[4:6, :] = lend_x[...].astype(F32)
+    wanted[...] = jnp.full(wanted.shape, -1, jnp.int32)
+    wanted[:, 0:face] = lend_y[1:2, :]
+    wanted[:, face : 2 * face] = lend_y[0:1, :]
+
+
+def pack_rows(coords, species, lend_x, lend_y):
+    atoms = coords.shape[1]
+    return pl.pallas_call(
+        pack_kernel,
+        out_shape=[edge_shape(8, atoms), jax.ShapeDtypeStruct((1, atoms), jnp.int32)],
+        in_specs=[WHOLE] * 4,
+        out_specs=[WHOLE] * 2,
+        compiler_params=params(),
+        name="pack_rows",
+    )(coords, species, lend_x, lend_y)
 
 
 def lend_rows(own, below, above, wanted):
@@ -388,15 +411,18 @@
     return (rows == index).astype(F32).astype(BF16)
 
 
-def mark_atoms(nbrs, unit, chosen):
-    start = pl.multiple_of(unit * UNIT, UNIT)
-    rows = lax.broadcasted_iota(jnp.int32, (UNIT, UNIT), 0)
-    centre = (rows == lax.broadcasted_iota(jnp.int32, (UNIT, UNIT), 1)).astype(F32)
+def mark_atoms(nbrs, unit, columns):
+    own = columns // 4
+    centre = lax.broadcasted_iota(jnp.int32, (1, UNIT), 1) + unit * UNIT
+    here = lax.broadcasted_iota(jnp.int32, (own, UNIT), 0)
+    away = lax.broadcasted_iota(jnp.int32, (columns - own, UNIT), 0) + own
+    parts = []
     for q in range(nbrs.shape[0]):
         index = nbrs[q : q + 1, :]
-        chosen[:, lanes_of(q)] = chosen_rows(index, chosen.shape[0], 0)
-        both = (rows + start == index).astype(F32) + centre
-        chosen[pl.ds(start, UNIT), lanes_of(q)] = both.astype(BF16)
+        top = (here == index).astype(F32) + (here == centre).astype(F32)
+        rest = (away == index).astype(F32)
+        parts.append(jnp.concatenate([top, rest], 0).astype(BF16))
+    return jnp.concatenate(parts, 1)
 
 
 def lend_env_kernel(wanted, *refs):
@@ -462,7 +488,7 @@
 
 def gathered(split, chosen, g):
     rows = HARM * TENSORS
-    both = dot(split[...], chosen[...])
+    both = dot(split[...], chosen)
     g[...] = both[:rows] + both[rows:]
 
 
@@ -482,7 +508,7 @@
 def middle_kernel(*refs, group, per, norm, count, aliased, first):
     geo, nbrs, x, lx, val, s_w, mix_w, cols = refs[:8]
     pieces = refs[8 : 8 + count]
-    g, slope_out, x_out, emb_out, val_out, lx_out, env_out, split, chosen = refs[
+    g, slope_out, x_out, emb_out, val_out, lx_out, env_out, split = refs[
         8 + count + aliased :
     ]
     step = pl.program_id(0)
@@ -491,7 +517,7 @@
     def _():
         fill_split(pieces, split)
 
-    mark_atoms(nbrs, first + step // per, chosen)
+    chosen = mark_atoms(nbrs, first + step // per, split.shape[1])
     gathered(split, chosen, g)
     s = contracted(geo, group, g, val[...])
     update, slope = silu_pair(lx[...] + product(s_w[0], s))
@@ -528,7 +554,6 @@
         + [unit_spec(HARM * TENSORS, per)],
         scratch_shapes=[
             pltpu.VMEM((2 * HARM * TENSORS, columns), BF16),
-            pltpu.VMEM((columns, group * UNIT), BF16),
         ],
         input_output_aliases={ins + n: n for n in range(len(before))},
         compiler_params=params(),
@@ -564,7 +589,7 @@
             dg[rows_of(m), span] = high
             dg[rows_of(HARM + m), span] = low
         columns.append(total)
-    both = dot_nt(dg[...], chosen[...])
+    both = dot_nt(dg[...], chosen)
     rows = HARM * TENSORS
     total = both[:rows] + both[rows:]
     wide[...] += total[:, : wide.shape[1]]
@@ -575,7 +600,7 @@
 def last_kernel(*refs, group, per, norm, count):
     geo, nbrs, x, lx, val, s_w, back_w, cols, base = refs[:9]
     pieces = refs[9 : 9 + count]
-    energy, esum, dx_out, dval_out, dgeo, wide, across, split, chosen, g, dg = refs[9 + count :]
+    energy, esum, dx_out, dval_out, dgeo, wide, across, split, g, dg = refs[9 + count :]
     step = pl.program_id(0)
 
     @pl.when(step == 0)
@@ -589,7 +614,7 @@
     def _():
         energy[...] = base[...]
 
-    mark_atoms(nbrs, step // per, chosen)
+    chosen = mark_atoms(nbrs, step // per, split.shape[1])
     gathered(split, chosen, g)
     value = val[...]
     s = contracted(geo, group, g, value)
@@ -652,7 +677,6 @@
         ],
         scratch_shapes=[
             pltpu.VMEM((2 * rows, columns), BF16),
-            pltpu.VMEM((columns, group * UNIT), BF16),
             pltpu.VMEM((rows, group * UNIT), F32),
             pltpu.VMEM((2 * rows, group * UNIT), BF16),
         ],
@@ -683,7 +707,7 @@
 def middle_back_kernel(*refs, group, per, norm, aliased, first):
     geo, nbrs, own, low, high, dgeo_in, dx, dval, emb, g, slope, val, ev_w, back_w = refs[:14]
     wide_in, across_in = refs[14:16] if aliased else (None, None)
-    dx_out, dval_out, dgeo, wide, across, total, chosen, dg = refs[14 + aliased :]
+    dx_out, dval_out, dgeo, wide, across, total, dg = refs[14 + aliased :]
     step = pl.program_id(0)
 
     @pl.when(step == 0)
@@ -695,7 +719,7 @@
     def _():
         total[...] = own[...] + low[...] + high[...]
 
-    mark_atoms(nbrs, first + step // per, chosen)
+    chosen = mark_atoms(nbrs, first + step // per, wide.shape[1] + across.shape[1])
     dgeo[...] = dgeo_in[...]
     demb = pull_env(geo, group, total, emb, dgeo, norm)
     d_fresh = dx[...] + product(ev_w[1], jnp.concatenate([demb, dval[...]], 0))
@@ -748,7 +772,6 @@
         ],
         scratch_shapes=[
             pltpu.VMEM((rows, UNIT), F32),
-            pltpu.VMEM((4 * atoms, group * UNIT), BF16),
             pltpu.VMEM((2 * rows, group * UNIT), BF16),
         ],
         input_output_aliases={16 + n: n for n in range(3)} if before else {},
@@ -901,17 +924,17 @@
     return pieces + [swap_y(lend_env(wanted, pieces), face)]
 
 
-def owned_grads(wide, across, wanted, face, widths, total, steps):
+def owned_grads(wide, across, wanted, face, widths, total, steps, hops):
     across, total = lax.optimization_barrier((across, total))
     returned = return_y(across, face)
-    total = sum_step(total, steps)
+    for _ in range(hops):
+        total = sum_step(total, steps)
     own, below, above = take_back(returned, wanted, wide, widths)
-    below[0], above[0], total = lax.optimization_barrier((below[0], above[0], total))
     found = []
     for number in range(len(widths)):
         send = below[number], above[number]
         if found:
-            send, found[-1] = lax.optimization_barrier((send, found[-1]))
+            send, found[-1], total = lax.optimization_barrier((send, found[-1], total))
         found.append(
             [own[number], passed_along(send[0], "gx", -1), passed_along(send[1], "gx", 1)]
         )
@@ -951,22 +974,7 @@
     nbrs = neighbours[0, 0]
     atoms = nbrs.shape[1]
     face = send_y.shape[3]
-    rows = jnp.concatenate(
-        [
-            positions[0, 0],
-            species[0, 0][None].astype(F32),
-            send_x[0, 0].astype(F32),
-            jnp.zeros((2, atoms), F32),
-        ],
-        0,
-    )
-    wanted = jnp.concatenate(
-        [
-            send_y[0, 0, 1],
-            send_y[0, 0, 0],
-            jnp.full((atoms - 2 * face,), -1, jnp.int32),
-        ]
-    )[None]
+    rows, wanted = pack_rows(positions[0, 0], species[0], send_x[0, 0], send_y[0, 0])
     below = passed_along(rows, "gx", 1)
     above = passed_along(rows, "gx", -1)
     two_w, mix_w, s_w, back_w, ev_w, rad_w, cols = prepare_weights(
@@ -999,7 +1007,7 @@
     steps = sum_steps()
     if steps is None:
         total = lax.psum(total, ("gx", "gy"))
-    grads, total = owned_grads(wide, across, wanted, face, (UNIT, atoms - UNIT), total, steps)
+    grads, total = owned_grads(wide, across, wanted, face, (UNIT, atoms - UNIT), total, steps, 1)
     before = []
     for number, span in enumerate(((0, 1), (1, units))):
         before = middle_back(
@@ -1007,7 +1015,7 @@
             slots, group, span, before,
         )
     dx, dval, dgeo, wide, across = before
-    grads, total = owned_grads(wide, across, wanted, face, (atoms - UNIT, UNIT), total, steps)
+    grads, total = owned_grads(wide, across, wanted, face, (atoms - UNIT, UNIT), total, steps, 2)
     before = []
     for number, span in enumerate(((0, units - 1), (units - 1, units))):
         before = [
@@ -1017,7 +1025,7 @@
             )
         ]
     wide, across = geometry_back(vec, before[0], nbrs, slots)
-    grads, total = owned_grads(wide, across, wanted, face, (atoms,), total, steps)
+    grads, total = owned_grads(wide, across, wanted, face, (atoms,), total, steps, 1)
     while steps:
         total = sum_step(total, steps)
     mean_energy = jnp.sum(total) / (atoms * lax.axis_size("gx") * lax.axis_size("gy"))

time: 389 us -> 320 us (0.82)
  Pallas kernels: 264 us -> 195 us
  starting transfers between devices: 33.4 us -> 46.2 us
  waiting for transfers between devices: 69.8 us -> 61 us
    pallas_call x1, Pallas kernels: 82.5 us -> 58.5 us  [last_pass(): pl.pallas_call(partial(last_kernel, group=group, per=per, norm=1.0 / math...]
    pallas_call x2, Pallas kernels: 64.2 us -> 40.9 us  [middle_pass(): pl.pallas_call(partial(middle_kernel, group=group, per=per, norm=1.0 / ma...]
    pallas_call x2, Pallas kernels: 65.9 us -> 43.3 us  [middle_back(): pl.pallas_call(partial(middle_back_kernel, group=group, per=per, norm=1.0...]
    ppermute x30, starting transfers between devices: 33.4 us -> 46.2 us  [passed_along(): lax.ppermute(value, axis, [(i, (i + by) % count) for i in range(count)])]
    ppermute x30, waiting for transfers between devices: 69.8 us -> 61 us  [passed_along(): lax.ppermute(value, axis, [(i, (i + by) % count) for i in range(count)])]
    unnamed x52 -> x50, local copies, waits for them, and re-layouts: 9.19 us -> 9.78 us
  transfers between devices with their start and end apart: 30 -> 30, of which waited for: 13 -> 16; matrix products, arithmetic and copies ran while one was open for 1% -> 0% of each run, Pallas kernels for 17% -> 16%
where the time goes in v1:
time: 320 us; the launch traced here: 317 us
  Pallas kernels  195 us (61%)
  waiting for transfers between devices  61 us (19%)
  starting transfers between devices  46.2 us (14%)
  local copies, waits for them, and re-layouts  9.78 us (3%)
    ppermute x30, waiting for transfers between devices, passed_along(): lax.ppermute(value, axis, [(i, (i + by) % count) for i in range(count)])  61 us
    pallas_call x1, Pallas kernels, last_pass(): pl.pallas_call(partial(last_kernel, group=group, per=per, norm=1.0 / math...  58.5 us
    ppermute x30, starting transfers between devices, passed_along(): lax.ppermute(value, axis, [(i, (i + by) % count) for i in range(count)])  46.2 us
    pallas_call x2, Pallas kernels, middle_back(): pl.pallas_call(partial(middle_back_kernel, group=group, per=per, norm=1.0...  43.3 us
    pallas_call x2, Pallas kernels, middle_pass(): pl.pallas_call(partial(middle_kernel, group=group, per=per, norm=1.0 / ma...  40.9 us
    pallas_call x2, Pallas kernels, first_pass(): pl.pallas_call(partial(first_kernel, group=group, per=per, norm=1.0 / mat...  13.4 us
    pallas_call x2, Pallas kernels, first_back(): pl.pallas_call(partial(first_back_kernel, group=group, per=per, norm=1.0...  12.6 us
    unnamed x50, local copies, waits for them, and re-layouts  9.78 us
  transfers between devices with their start and end apart: 30, of which 16 were waited for; matrix products, arithmetic and copies ran while one was open for 0% of the time, Pallas kernels for 16%

profile of v1, /device:TPU:0, one launch (start us, length us, event | category | flops | bytes accessed | tf_op | source)
XLA Modules:
  0.0 317.1 jit_solution(5222399525012261150)
XLA Ops:
  3.3 6.0 %collective-permute-start.1 = (f32[8,384]{1,0:T(8,128)}, f32[8,384]{1,0:T(8,128)S(1)}, u32[]{:S(2)}, u32[]{:S(2)}) collective-permute-start(f32[8,384]{1,0:T(8,128)} %get-tuple-element.102.own), channel_id=1, source_target_pairs={{0,14},{2,0},{4,2},{6,4},{8,6},{10,8},{12,10},{14,12},{1,15},{3,1}... | collective-permute-start | bytes 36872 | tf_op jit(solution)/shard_map/ppermute | solution.py:34
  10.9 5.0 %collective-permute-done.below = f32[8,384]{1,0:T(8,128)S(1)} collective-permute-done((f32[8,384]{1,0:T(8,128)}, f32[8,384]{1,0:T(8,128)S(1)}, u32[]{:S(2)}, u32[]{:S(2)}) %collective-permute-start) | collective-permute-done | bytes 12320 | tf_op jit(solution)/shard_map/ppermute | solution.py:34
  18.0 2.2 prepare_weights.1
  20.8 3.5 %geometry.1 = (f32[3,96,128]{2,1,0:T(8,128)}, f32[18,96,128]{2,1,0:T(8,128)}, s32[96,128]{1,0:T(8,128)}, f32[1,384]{1,0:T(1,128)}) custom-call(f32[8,384]{1,0:T(8,128)} %get-tuple-element.102.own, f32[8,384]{1,0:T(8,128)} %copy-done.14, f32[8,384]{1,0:T(8,128)} %copy-done.13, f32[8,384]{1,0:T(8,128)} %copy-done.15, s32[32,384]{1,0:T(8,128)} %bitcast.15, f32[5]{0:T(128)} %shift.1), custom_call_target="tpu_custom_call" | custom-call | tf_op jit(solution)/shard_map/geometry/pallas_call | solution.py:294
  24.3 5.3 %first_pass.2 = (f32[128,12288]{1,0:T(8,128)}, f32[128,12288]{1,0:T(8,128)}, f32[32,12288]{1,0:T(8,128)}, f32[32,12288]{1,0:T(8,128)}, f32[128,12288]{1,0:T(8,128)}, /*index=5*/f32[288,128]{1,0:T(8,128)}) custom-call(f32[18,96,128]{2,1,0:T(8,128)} %get-tuple-element.105.geo.refs_0_, f32[8,384]{1,0:T(8,128)} %get-tuple-element.102.own, ...), custom_call_target="tpu_custom_call" | custom-call | flops 12884901888 | bytes 25165824 | tf_op jit(solution)/shard_map/first_pass/pallas_call | solution.py:392
  31.7 8.2 %first_pass.3 = (f32[128,12288]{1,0:T(8,128)}, f32[128,12288]{1,0:T(8,128)}, f32[32,12288]{1,0:T(8,128)}, f32[32,12288]{1,0:T(8,128)}, f32[128,12288]{1,0:T(8,128)}, /*index=5*/f32[288,256]{1,0:T(8,128)}) custom-call(f32[18,96,128]{2,1,0:T(8,128)} %get-tuple-element.105.geo.refs_0_, ...), custom_call_target="tpu_custom_call", output_to_operand_aliasing={{0}: (5, {}), {1}: (6, {}), {2}: (7, {}), {3}: (8, {}), {4}... | custom-call | flops 12884901888 | bytes 25165824 | tf_op jit(solution)/shard_map/first_pass/pallas_call | solution.py:392
  39.9 2.8 collective-permute-start.6
  42.7 12.6 %collective-permute-done.6.refs_5_.refs_13_ = f32[288,256]{1,0:T(8,128)S(1)} collective-permute-done((f32[288,256]{1,0:T(8,128)}, f32[288,256]{1,0:T(8,128)S(1)}, u32[]{:S(2)}, u32[]{:S(2)}) %collective-permute-start.6) | collective-permute-done | bytes 294944 | tf_op jit(solution)/shard_map/ppermute | solution.py:34
  56.1 3.1 lend_env.2
  62.0 25.5 %middle_pass.2 = (f32[288,12288]{1,0:T(8,128)}, f32[128,12288]{1,0:T(8,128)}, f32[128,12288]{1,0:T(8,128)}, f32[32,12288]{1,0:T(8,128)}, f32[32,12288]{1,0:T(8,1...) custom-call(f32[18,96,128]{2,1,0:T(8,128)} %get-tuple-element.105.geo.refs_0_, s32[96,128]{1,0:T(8,128)} %get-tuple-element.106.refs_1_.nbrs, ...), custom_call_target="tpu_custom_call" | custom-call | flops 10871635968 | bytes 21233664 | tf_op jit(solution)/shard_map/middle_pass/pallas_call | solution.py:541
  87.6 3.1 collective-permute-start.9
  90.6 10.3 %collective-permute-start.8 = (f32[288,256]{1,0:T(8,128)}, f32[288,256]{1,0:T(8,128)S(1)}, u32[]{:S(2)}, u32[]{:S(2)}) collective-permute-start(f32[288,256]{1,0:T(8,128)} %get-tuple-element.136.refs_0_.refs_9_), channel_id=1, source_target_pairs={{0,2},{2,4},{4,6},{6,8},{8,10},{10,12},{12,14},{14,0},{1,3},{3,5},... | collective-permute-start | bytes 884744 | tf_op jit(solution)/shard_map/ppermute | solution.py:34
  100.9 15.4 %middle_pass.3 = (f32[288,12288]{1,0:T(8,128)}, f32[128,12288]{1,0:T(8,128)}, f32[128,12288]{1,0:T(8,128)}, f32[32,12288]{1,0:T(8,128)}, f32[32,12288]{1,0:T(8,1...) custom-call(f32[18,96,128]{2,1,0:T(8,128)} %get-tuple-element.105.ge, ...), custom_call_target="tpu_custom_call", output_to_operand_aliasing={{0}: (15, {}), {1}: (16, {}), {2}: (17, {}), {3}: (18, {}),... | custom-call | flops 10871635968 | bytes 21233664 | tf_op jit(solution)/shard_map/middle_pass/pallas_call | solution.py:541
  116.3 4.7 %collective-permute-start.11 = (f32[288,128]{1,0:T(8,128)}, f32[288,128]{1,0:T(8,128)S(1)}, u32[]{:S(2)}, u32[]{:S(2)}) collective-permute-start(f32[288,128]{1,0:T(8,128)} %get-tuple-element.139.refs_1_.refs_10_), channel_id=1, source_target_pairs={{0,14},{2,0},{4,2},{6,4},{8,6},{10,8},{12,10},{14,12},{1,15},{3,1}... | collective-permute-start | bytes 442376 | tf_op jit(solution)/shard_map/ppermute | solution.py:34
  121.1 3.2 collective-permute-done.11.refs_5_.refs_14_
  124.2 4.9 %collective-permute-done.10.refs_3_.refs_12_ = f32[288,128]{1,0:T(8,128)S(1)} collective-permute-done((f32[288,128]{1,0:T(8,128)}, f32[288,128]{1,0:T(8,128)S(1)}, u32[]{:S(2)}, u32[]{:S(2)}) %collective-permute-start.10) | collective-permute-done | bytes 147488 | tf_op jit(solution)/shard_map/ppermute | solution.py:34
  129.8 3.0 lend_env.3
  135.6 58.5 %last_pass.1 = (f32[1,384]{1,0:T(1,128)}, f32[8,128]{1,0:T(8,128)}, f32[128,12288]{1,0:T(8,128)}, f32[32,12288]{1,0:T(8,128)}, f32[9,96,128]{2,1,0:T(8,128)}, /*index=5*/f32[288,1152]{1,0:T(8,128)}, f32[288,384]{1,0:T(8,128)}) custom-call(f32[18,96,128]{2,1,0:T(8,128)} %get-tuple-element.105.geo.refs_0_, s32[96,128]{1,0:T(8,128)} %get-tuple-element.106.refs_1_.nbrs, ...), custom_call_target="tpu_custom_call" | custom-call | flops 21743271936 | bytes 42467328 | tf_op jit(solution)/shard_map/last_pass/pallas_call | solution.py:650
  196.9 3.2 %take_back.3 = (f32[288,128]{1,0:T(8,128)}, f32[288,256]{1,0:T(8,128)}, f32[288,128]{1,0:T(8,128)}, f32[288,256]{1,0:T(8,128)}, f32[288,128]{1,0:T(8,128)}, /*index=5*/f32[288,256]{1,0:T(8,128)}) custom-call(f32[288,384]{1,0:T(8,128)} %copy-done.5, s32[1,384]{1,0:T(1,128)} %get-tuple-element.124.wanted, f32[288,1152]{1,0:T(8,128)} %get-tuple-element.146.wide), custom_call_target="tpu_custom_call" | custom-call | tf_op jit(solution)/shard_map/take_back/pallas_call | solution.py:466
  202.2 7.5 %collective-permute-done.16 = f32[8,128]{1,0:T(8,128)S(1)} collective-permute-done((f32[8,128]{1,0:T(8,128)}, f32[8,128]{1,0:T(8,128)S(1)}, u32[]{:S(2)}, u32[]{:S(2)}) %collective-permute-start.16) | collective-permute-done | bytes 4128 | tf_op jit(solution)/shard_map/ppermute | solution.py:34
  212.5 15.6 %middle_back.2 = (f32[128,12288]{1,0:T(8,128)}, f32[32,12288]{1,0:T(8,128)}, f32[9,96,128]{2,1,0:T(8,128)}, f32[288,1152]{1,0:T(8,128)}, f32[288,384]{1,0:T(8,128)}) custom-call(f32[18,96,128]{2,1,0:T(8,128)} %get-tuple-element.105.geo.refs_0_, s32[96,128]{1,0:T(8,128)} %get-tuple-element.106.refs_1_.nbrs, f32[288,128]{1,0:T(8,128)} %get-tuple-element.163.refs_2_, ...), custom_call_target="tpu_custom_call" | custom-call | flops 10871635968 | bytes 21233664 | tf_op jit(solution)/shard_map/middle_back/pallas_call | solution.py:750
  229.0 27.6 %middle_back.3 = (f32[128,12288]{1,0:T(8,128)}, f32[32,12288]{1,0:T(8,128)}, f32[9,96,128]{2,1,0:T(8,128)}, f32[288,1152]{1,0:T(8,128)}, f32[288,384]{1,0:T(8,128)}) custom-call(f32[18,96,128]{2,1,0:T(8,128)} %get-tuple-element.105.geo.refs_0_, ...), custom_call_target="tpu_custom_call", output_to_operand_aliasing={{0}: (16, {}), {1}: (17, {}), {2}: (18, {})} | custom-call | flops 10871635968 | bytes 21233664 | tf_op jit(solution)/shard_map/middle_back/pallas_call | solution.py:750
  259.5 3.3 %take_back.4 = (f32[288,256]{1,0:T(8,128)}, f32[288,128]{1,0:T(8,128)}, f32[288,256]{1,0:T(8,128)}, f32[288,128]{1,0:T(8,128)}, f32[288,256]{1,0:T(8,128)}, /*index=5*/f32[288,128]{1,0:T(8,128)}) custom-call(f32[288,384]{1,0:T(8,128)} %copy-done.6, s32[1,384]{1,0:T(1,128)} %get-tuple-element.124.wanted, f32[288,1152]{1,0:T(8,128)} %get-tuple-element.174.wide), custom_call_target="tpu_custom_call" | custom-call | tf_op jit(solution)/shard_map/take_back/pallas_call | solution.py:466
  262.7 3.5 %collective-permute-start.20 = (f32[288,256]{1,0:T(8,128)}, f32[288,256]{1,0:T(8,128)S(1)}, u32[]{:S(2)}, u32[]{:S(2)}) collective-permute-start(f32[288,256]{1,0:T(8,128)} %get-tuple-element.179), channel_id=1, source_target_pairs={{0,14},{2,0},{4,2},{6,4},{8,6},{10,8},{12,10},{14,12},{1,15},{3,1}... | collective-permute-start | bytes 884744 | tf_op jit(solution)/shard_map/ppermute | solution.py:34
  266.2 7.0 %collective-permute-done.22 = f32[8,128]{1,0:T(8,128)S(1)} collective-permute-done((f32[8,128]{1,0:T(8,128)S(1)}, f32[8,128]{1,0:T(8,128)S(1)}, u32[]{:S(2)}, u32[]{:S(2)}) %collective-permute-start.22) | collective-permute-done | bytes 4128 | tf_op jit(solution)/shard_map/ppermute | solution.py:34
  273.2 4.5 %collective-permute-done.23 = f32[8,128]{1,0:T(8,128)S(1)} collective-permute-done((f32[8,128]{1,0:T(8,128)S(1)}, f32[8,128]{1,0:T(8,128)S(1)}, u32[]{:S(2)}, u32[]{:S(2)}) %collective-permute-start.23) | collective-permute-done | bytes 4128 | tf_op jit(solution)/shard_map/ppermute | solution.py:34
  278.3 3.9 %collective-permute-start.24 = (f32[288,128]{1,0:T(8,128)}, f32[288,128]{1,0:T(8,128)S(1)}, u32[]{:S(2)}, u32[]{:S(2)}) collective-permute-start(f32[288,128]{1,0:T(8,128)} %get-tuple-element.182), channel_id=1, source_target_pairs={{0,14},{2,0},{4,2},{6,4},{8,6},{10,8},{12,10},{14,12},{1,15},{3,1}... | collective-permute-start | bytes 442376 | tf_op jit(solution)/shard_map/ppermute | solution.py:34
  283.5 7.9 %first_back.2.rest_0_ = f32[17,96,128]{2,1,0:T(8,128)} custom-call(f32[18,96,128]{2,1,0:T(8,128)} %get-tuple-element.105.geo.refs_0_, f32[288,256]{1,0:T(8,128)} %get-tuple-element.190.own, f32[288,256]{1,0:T(8,128)} %copy-done.18, f32[288,256]{1,0:T(8,128)} %copy-done.19, f32[9,96,128]{2,1,0:T(8,128)} %get-tuple-element.184.dgeo_in, ...), custom_call_target="tpu_custom_call" | custom-call | flops 12884901888 | bytes 25165824 | tf_op jit(solution)/shard_map/first_back/pallas_call | solution.py:809
  292.1 4.7 %first_back.3.dgeo = f32[17,96,128]{2,1,0:T(8,128)} custom-call(f32[18,96,128]{2,1,0:T(8,128)} %get-tuple-element.105.geo.refs_0_, f32[288,128]{1,0:T(8,128)} %get-tuple-element.175.own, f32[288,128]{1,0:T(8,128)} %copy-done.22, f32[288,128]{1,0:T(8,128)} %copy-done.23, f32[9,96,128]{2,1,0:T(8,128)} %get-tuple-element.184.dgeo_in, ...), custom_call_target="tpu_custom_call", output_to_operand_aliasing={{}: (11, {})} | custom-call | flops 12884901888 | bytes 25165824 | tf_op jit(solution)/shard_map/first_back/pallas_call | solution.py:809
  296.8 3.4 %geometry_back.1 = (f32[8,1152]{1,0:T(8,128)}, f32[8,384]{1,0:T(8,128)}) custom-call(f32[3,96,128]{2,1,0:T(8,128)} %get-tuple-element.142.vec, f32[17,96,128]{2,1,0:T(8,128)} %first_back.3.dgeo, s32[96,128]{1,0:T(8,128)} %get-tuple-element.106.refs_1_.nbrs), custom_call_target="tpu_custom_call" | custom-call | tf_op jit(solution)/shard_map/geometry_back/pallas_call | solution.py:889
  304.0 3.7 %collective-permute-start.27 = (f32[8,384]{1,0:T(8,128)}, f32[8,384]{1,0:T(8,128)S(1)}, u32[]{:S(2)}, u32[]{:S(2)}) collective-permute-start(f32[8,384]{1,0:T(8,128)} %get-tuple-element.198), channel_id=1, source_target_pairs={{0,14},{2,0},{4,2},{6,4},{8,6},{10,8},{12,10},{14,12},{1,15},{3,1}... | collective-permute-start | bytes 36872 | tf_op jit(solution)/shard_map/ppermute | solution.py:34
  309.3 5.0 %collective-permute-done.28 = f32[8,384]{1,0:T(8,128)S(1)} collective-permute-done((f32[8,384]{1,0:T(8,128)}, f32[8,384]{1,0:T(8,128)S(1)}, u32[]{:S(2)}, u32[]{:S(2)}) %collective-permute-start.28) | collective-permute-done | bytes 12320 | tf_op jit(solution)/shard_map/ppermute | solution.py:34
  (102 shorter events, 36.2 us)
Async XLA Ops:
  3.3 7.6 %collective-permute-start.1 = (f32[8,384]{1,0:T(8,128)}, f32[8,384]{1,0:T(8,128)S(1)}, u32[]{:S(2)}, u32[]{:S(2)}) collective-permute-start(f32[8,384]{1,0:T(8,128)} %get-tuple-element.102.own), channel_id=1, source_target_pairs={{0,14},{2,0},{4,2},{6,4},{8,6},{10,8},{12,10},{14,12},{1,15},{3,1}... | collective-permute-start | bytes 36872 | tf_op jit(solution)/shard_map/ppermute | solution.py:34
  9.3 6.6 %collective-permute-start = (f32[8,384]{1,0:T(8,128)}, f32[8,384]{1,0:T(8,128)S(1)}, u32[]{:S(2)}, u32[]{:S(2)}) collective-permute-start(f32[8,384]{1,0:T(8,128)} %get-tuple-element.102.own), channel_id=1, source_target_pairs={{0,2},{2,4},{4,6},{6,8},{8,10},{10,12},{12,14},{14,0},{1,3},{3,5},... | collective-permute-start | bytes 36872 | tf_op jit(solution)/shard_map/ppermute | solution.py:34
  18.0 2.2 collective-permute-start.2
  29.6 10.2 %collective-permute-start.4 = (f32[288,128]{1,0:T(8,128)}, f32[288,128]{1,0:T(8,128)S(1)}, u32[]{:S(2)}, u32[]{:S(2)}) collective-permute-start(f32[288,128]{1,0:T(8,128)} %get-tuple-element.119.refs_0_.refs_8_), channel_id=1, source_target_pairs={{0,14},{2,0},{4,2},{6,4},{8,6},{10,8},{12,10},{14,12},{1,15},{3,1}... | collective-permute-start | bytes 442376 | tf_op jit(solution)/shard_map/ppermute | solution.py:34
  29.7 10.2 %collective-permute-start.3 = (f32[288,128]{1,0:T(8,128)}, f32[288,128]{1,0:T(8,128)S(1)}, u32[]{:S(2)}, u32[]{:S(2)}) collective-permute-start(f32[288,128]{1,0:T(8,128)} %get-tuple-element.119.refs_0_.refs_8_), channel_id=1, source_target_pairs={{0,2},{2,4},{4,6},{6,8},{8,10},{10,12},{12,14},{14,0},{1,3},{3,5},... | collective-permute-start | bytes 442376 | tf_op jit(solution)/shard_map/ppermute | solution.py:34
  39.8 15.5 %copy-start.2 = (f32[288,128]{1,0:T(8,128)}, f32[288,128]{1,0:T(8,128)S(1)}, u32[]{:S(2)}) copy-start(f32[288,128]{1,0:T(8,128)S(1)} %collective-permute-done.4.refs_4_.refs_12_) | copy-start | bytes 442372
  39.9 15.5 %copy-start.3 = (f32[288,128]{1,0:T(8,128)}, f32[288,128]{1,0:T(8,128)S(1)}, u32[]{:S(2)}) copy-start(f32[288,128]{1,0:T(8,128)S(1)} %collective-permute-done.3.refs_2_.refs_10_) | copy-start | bytes 442372
  39.9 15.4 %collective-permute-start.6 = (f32[288,256]{1,0:T(8,128)}, f32[288,256]{1,0:T(8,128)S(1)}, u32[]{:S(2)}, u32[]{:S(2)}) collective-permute-start(f32[288,256]{1,0:T(8,128)} %get-tuple-element.122.refs_1_.refs_9_), channel_id=1, source_target_pairs={{0,14},{2,0},{4,2},{6,4},{8,6},{10,8},{12,10},{14,12},{1,15},{3,1}... | collective-permute-start | bytes 884744 | tf_op jit(solution)/shard_map/ppermute | solution.py:34
  42.7 12.6 %collective-permute-start.5 = (f32[288,256]{1,0:T(8,128)}, f32[288,256]{1,0:T(8,128)S(1)}, u32[]{:S(2)}, u32[]{:S(2)}) collective-permute-start(f32[288,256]{1,0:T(8,128)} %get-tuple-element.122.refs_1_.refs_9_), channel_id=1, source_target_pairs={{0,2},{2,4},{4,6},{6,8},{8,10},{10,12},{12,14},{14,0},{1,3},{3,5},... | collective-permute-start | bytes 884744 | tf_op jit(solution)/shard_map/ppermute | solution.py:34
  59.2 2.0 collective-permute-start.7
  87.6 28.8 %collective-permute-start.9 = (f32[288,256]{1,0:T(8,128)}, f32[288,256]{1,0:T(8,128)S(1)}, u32[]{:S(2)}, u32[]{:S(2)}) collective-permute-start(f32[288,256]{1,0:T(8,128)} %get-tuple-element.136.refs_0_.refs_9_), channel_id=1, source_target_pairs={{0,14},{2,0},{4,2},{6,4},{8,6},{10,8},{12,10},{14,12},{1,15},{3,1}... | collective-permute-start | bytes 884744 | tf_op jit(solution)/shard_map/ppermute | solution.py:34
  90.6 25.7 %collective-permute-start.8 = (f32[288,256]{1,0:T(8,128)}, f32[288,256]{1,0:T(8,128)S(1)}, u32[]{:S(2)}, u32[]{:S(2)}) collective-permute-start(f32[288,256]{1,0:T(8,128)} %get-tuple-element.136.refs_0_.refs_9_), channel_id=1, source_target_pairs={{0,2},{2,4},{4,6},{6,8},{8,10},{10,12},{12,14},{14,0},{1,3},{3,5},... | collective-permute-start | bytes 884744 | tf_op jit(solution)/shard_map/ppermute | solution.py:34
  116.3 7.9 %collective-permute-start.11 = (f32[288,128]{1,0:T(8,128)}, f32[288,128]{1,0:T(8,128)S(1)}, u32[]{:S(2)}, u32[]{:S(2)}) collective-permute-start(f32[288,128]{1,0:T(8,128)} %get-tuple-element.139.refs_1_.refs_10_), channel_id=1, source_target_pairs={{0,14},{2,0},{4,2},{6,4},{8,6},{10,8},{12,10},{14,12},{1,15},{3,1}... | collective-permute-start | bytes 442376 | tf_op jit(solution)/shard_map/ppermute | solution.py:34
  121.1 8.1 %collective-permute-start.10 = (f32[288,128]{1,0:T(8,128)}, f32[288,128]{1,0:T(8,128)S(1)}, u32[]{:S(2)}, u32[]{:S(2)}) collective-permute-start(f32[288,128]{1,0:T(8,128)} %get-tuple-element.139.refs_1_.refs_10_), channel_id=1, source_target_pairs={{0,2},{2,4},{4,6},{6,8},{8,10},{10,12},{12,14},{14,0},{1,3},{3,5},... | collective-permute-start | bytes 442376 | tf_op jit(solution)/shard_map/ppermute | solution.py:34
  132.8 2.0 collective-permute-start.12
  194.1 2.1 collective-permute-start.13
  200.1 10.2 %collective-permute-start.14 = (f32[288,128]{1,0:T(8,128)}, f32[288,128]{1,0:T(8,128)S(1)}, u32[]{:S(2)}, u32[]{:S(2)}) collective-permute-start(f32[288,128]{1,0:T(8,128)} %get-tuple-element.151), channel_id=1, source_target_pairs={{0,14},{2,0},{4,2},{6,4},{8,6},{10,8},{12,10},{14,12},{1,15},{3,1}... | collective-permute-start | bytes 442376 | tf_op jit(solution)/shard_map/ppermute | solution.py:34
  201.1 9.3 %collective-permute-start.15 = (f32[288,128]{1,0:T(8,128)}, f32[288,128]{1,0:T(8,128)S(1)}, u32[]{:S(2)}, u32[]{:S(2)}) collective-permute-start(f32[288,128]{1,0:T(8,128)} %get-tuple-element.152), channel_id=1, source_target_pairs={{0,2},{2,4},{4,6},{6,8},{8,10},{10,12},{12,14},{14,0},{1,3},{3,5},... | collective-permute-start | bytes 442376 | tf_op jit(solution)/shard_map/ppermute | solution.py:34
  202.2 7.5 %collective-permute-start.16 = (f32[8,128]{1,0:T(8,128)}, f32[8,128]{1,0:T(8,128)S(1)}, u32[]{:S(2)}, u32[]{:S(2)}) collective-permute-start(f32[8,128]{1,0:T(8,128)} %get-tuple-element.153), channel_id=1, source_target_pairs={{0,2},{2,4},{4,6},{6,8},{8,10},{10,12},{12,14},{14,0},{1,3},{3,5},... | collective-permute-start | bytes 12296 | tf_op jit(solution)/shard_map/ppermute | solution.py:34
  210.4 17.7 %collective-permute-start.17 = (f32[288,256]{1,0:T(8,128)}, f32[288,256]{1,0:T(8,128)S(1)}, u32[]{:S(2)}, u32[]{:S(2)}) collective-permute-start(f32[288,256]{1,0:T(8,128)} %get-tuple-element.154), channel_id=1, source_target_pairs={{0,14},{2,0},{4,2},{6,4},{8,6},{10,8},{12,10},{14,12},{1,15},{3,1}... | collective-permute-start | bytes 884744 | tf_op jit(solution)/shard_map/ppermute | solution.py:34
  211.2 16.9 %collective-permute-start.18 = (f32[288,256]{1,0:T(8,128)}, f32[288,256]{1,0:T(8,128)S(1)}, u32[]{:S(2)}, u32[]{:S(2)}) collective-permute-start(f32[288,256]{1,0:T(8,128)} %get-tuple-element.155), channel_id=1, source_target_pairs={{0,2},{2,4},{4,6},{6,8},{8,10},{10,12},{12,14},{14,0},{1,3},{3,5},... | collective-permute-start | bytes 884744 | tf_op jit(solution)/shard_map/ppermute | solution.py:34
  256.6 2.1 collective-permute-start.19
  262.7 15.6 %collective-permute-start.20 = (f32[288,256]{1,0:T(8,128)}, f32[288,256]{1,0:T(8,128)S(1)}, u32[]{:S(2)}, u32[]{:S(2)}) collective-permute-start(f32[288,256]{1,0:T(8,128)} %get-tuple-element.179), channel_id=1, source_target_pairs={{0,14},{2,0},{4,2},{6,4},{8,6},{10,8},{12,10},{14,12},{1,15},{3,1}... | collective-permute-start | bytes 884744 | tf_op jit(solution)/shard_map/ppermute | solution.py:34
  266.2 12.1 %collective-permute-start.21 = (f32[288,256]{1,0:T(8,128)}, f32[288,256]{1,0:T(8,128)S(1)}, u32[]{:S(2)}, u32[]{:S(2)}) collective-permute-start(f32[288,256]{1,0:T(8,128)} %get-tuple-element.180), channel_id=1, source_target_pairs={{0,2},{2,4},{4,6},{6,8},{8,10},{10,12},{12,14},{14,0},{1,3},{3,5},... | collective-permute-start | bytes 884744 | tf_op jit(solution)/shard_map/ppermute | solution.py:34
  266.2 7.0 %collective-permute-start.22 = (f32[8,128]{1,0:T(8,128)S(1)}, f32[8,128]{1,0:T(8,128)S(1)}, u32[]{:S(2)}, u32[]{:S(2)}) collective-permute-start(f32[8,128]{1,0:T(8,128)S(1)} %add.18), channel_id=1, source_target_pairs={{0,4},{2,6},{4,8},{6,10},{8,12},{10,14},{12,0},{14,2},{1,5},{3,7},... | collective-permute-start | bytes 12296 | tf_op jit(solution)/shard_map/ppermute | solution.py:34
  273.2 4.5 %collective-permute-start.23 = (f32[8,128]{1,0:T(8,128)S(1)}, f32[8,128]{1,0:T(8,128)S(1)}, u32[]{:S(2)}, u32[]{:S(2)}) collective-permute-start(f32[8,128]{1,0:T(8,128)S(1)} %add.19), channel_id=1, source_target_pairs={{0,8},{2,10},{4,12},{6,14},{8,0},{10,2},{12,4},{14,6},{1,9},{3,11}... | collective-permute-start | bytes 12296 | tf_op jit(solution)/shard_map/ppermute | solution.py:34
  278.3 13.0 %collective-permute-start.24 = (f32[288,128]{1,0:T(8,128)}, f32[288,128]{1,0:T(8,128)S(1)}, u32[]{:S(2)}, u32[]{:S(2)}) collective-permute-start(f32[288,128]{1,0:T(8,128)} %get-tuple-element.182), channel_id=1, source_target_pairs={{0,14},{2,0},{4,2},{6,4},{8,6},{10,8},{12,10},{14,12},{1,15},{3,1}... | collective-permute-start | bytes 442376 | tf_op jit(solution)/shard_map/ppermute | solution.py:34
  282.2 9.2 %collective-permute-start.25 = (f32[288,128]{1,0:T(8,128)}, f32[288,128]{1,0:T(8,128)S(1)}, u32[]{:S(2)}, u32[]{:S(2)}) collective-permute-start(f32[288,128]{1,0:T(8,128)} %get-tuple-element.183), channel_id=1, source_target_pairs={{0,2},{2,4},{4,6},{6,8},{8,10},{10,12},{12,14},{14,0},{1,3},{3,5},... | collective-permute-start | bytes 442376 | tf_op jit(solution)/shard_map/ppermute | solution.py:34
  300.2 1.4 collective-permute-start.26
  300.2 7.4 %collective-permute-start.29 = (f32[8,128]{1,0:T(8,128)S(1)}, f32[8,128]{1,0:T(8,128)S(1)}, u32[]{:S(2)}, u32[]{:S(2)}) collective-permute-start(f32[8,128]{1,0:T(8,128)S(1)} %add.20), channel_id=1, source_target_pairs={{0,1},{1,0},{2,3},{3,2},{4,5},{5,4},{6,7},{7,6},{8,9},{9,8},{10,11... | collective-permute-start | bytes 12296 | tf_op jit(solution)/shard_map/ppermute | solution.py:34
  304.0 5.3 %collective-permute-start.27 = (f32[8,384]{1,0:T(8,128)}, f32[8,384]{1,0:T(8,128)S(1)}, u32[]{:S(2)}, u32[]{:S(2)}) collective-permute-start(f32[8,384]{1,0:T(8,128)} %get-tuple-element.198), channel_id=1, source_target_pairs={{0,14},{2,0},{4,2},{6,4},{8,6},{10,8},{12,10},{14,12},{1,15},{3,1}... | collective-permute-start | bytes 36872 | tf_op jit(solution)/shard_map/ppermute | solution.py:34
  307.7 6.6 %collective-permute-start.28 = (f32[8,384]{1,0:T(8,128)}, f32[8,384]{1,0:T(8,128)S(1)}, u32[]{:S(2)}, u32[]{:S(2)}) collective-permute-start(f32[8,384]{1,0:T(8,128)} %get-tuple-element.199), channel_id=1, source_target_pairs={{0,2},{2,4},{4,6},{6,8},{8,10},{10,12},{12,14},{14,0},{1,3},{3,5},... | collective-permute-start | bytes 36872 | tf_op jit(solution)/shard_map/ppermute | solution.py:34
  (22 other events, 60.0 us)

commit v2 on v1

--- a/solution.py
+++ b/solution.py
@@ -26,7 +26,7 @@
 
 
 def params():
-    return pltpu.CompilerParams(vmem_limit_bytes=60 << 20)
+    return pltpu.CompilerParams(vmem_limit_bytes=44 << 20)
 
 
 def passed_along(value, axis, by):

time: 320 us -> 286 us (0.89)
  Pallas kernels: 195 us -> 164 us
    pallas_call x3, Pallas kernels: 8.25 us -> 2.33 us  [take_back(): pl.pallas_call(partial(take_back_kernel, widths=widths), out_shape=[edge_...]
    pallas_call x2, Pallas kernels: 6.13 us -> 1.96 us  [lend_env(): pl.pallas_call(lend_env_kernel, out_shape=jax.ShapeDtypeStruct((HARM * TE...]
    pallas_call x2, Pallas kernels: 43.3 us -> 39.4 us  [middle_back(): pl.pallas_call(partial(middle_back_kernel, group=group, per=per, norm=1.0...]
    unnamed x50 -> x30, local copies, waits for them, and re-layouts: 9.78 us -> 9.93 us
  transfers between devices with their start and end apart: 30 -> 30, of which waited for: 16 -> 18; matrix products, arithmetic and copies ran while one was open for 0% -> 0% of each run, Pallas kernels for 16% -> 15%
where the time goes in v2:
time: 286 us; the launch traced here: 282 us
  Pallas kernels  164 us (57%)
  waiting for transfers between devices  59.5 us (21%)
  starting transfers between devices  45.5 us (16%)
  local copies, waits for them, and re-layouts  9.93 us (3%)
  between operations  3.11 us (1%)
    ppermute x30, waiting for transfers between devices, passed_along(): lax.ppermute(value, axis, [(i, (i + by) % count) for i in range(count)])  59.5 us
    pallas_call x1, Pallas kernels, last_pass(): pl.pallas_call(partial(last_kernel, group=group, per=per, norm=1.0 / math...  56.4 us
    ppermute x30, starting transfers between devices, passed_along(): lax.ppermute(value, axis, [(i, (i + by) % count) for i in range(count)])  45.5 us
    pallas_call x2, Pallas kernels, middle_back(): pl.pallas_call(partial(middle_back_kernel, group=group, per=per, norm=1.0...  39.4 us
    pallas_call x2, Pallas kernels, middle_pass(): pl.pallas_call(partial(middle_kernel, group=group, per=per, norm=1.0 / ma...  38.7 us
    pallas_call x2, Pallas kernels, first_pass(): pl.pallas_call(partial(first_kernel, group=group, per=per, norm=1.0 / mat...  10.7 us
    pallas_call x2, Pallas kernels, first_back(): pl.pallas_call(partial(first_back_kernel, group=group, per=per, norm=1.0...  9.96 us
    unnamed x30, local copies, waits for them, and re-layouts  9.93 us
  transfers between devices with their start and end apart: 30, of which 18 were waited for; matrix products, arithmetic and copies ran while one was open for 0% of the time, Pallas kernels for 15%

profile of v2, /device:TPU:0, one launch (start us, length us, event | category | flops | bytes accessed | tf_op | source)
XLA Modules:
  0.0 282.5 jit_solution(14295864717520030411)
XLA Ops:
  3.4 6.0 %collective-permute-start.1 = (f32[8,384]{1,0:T(8,128)S(1)}, f32[8,384]{1,0:T(8,128)S(1)}, u32[]{:S(2)}, u32[]{:S(2)}) collective-permute-start(f32[8,384]{1,0:T(8,128)S(1)} %get-tuple-element.102.own), channel_id=1, source_target_pairs={{0,14},{2,0},{4,2},{6,4},{8,6},{10,8},{12,10},{14,12},{1,15},{3,1}... | collective-permute-start | bytes 36872 | tf_op jit(solution)/shard_map/ppermute | solution.py:34
  10.8 5.0 %collective-permute-done.below = f32[8,384]{1,0:T(8,128)S(1)} collective-permute-done((f32[8,384]{1,0:T(8,128)S(1)}, f32[8,384]{1,0:T(8,128)S(1)}, u32[]{:S(2)}, u32[]{:S(2)}) %collective-permute-start) | collective-permute-done | bytes 12320 | tf_op jit(solution)/shard_map/ppermute | solution.py:34
  23.0 2.3 geometry.1
  25.3 4.0 %first_pass.2 = (f32[128,12288]{1,0:T(8,128)}, f32[128,12288]{1,0:T(8,128)}, f32[32,12288]{1,0:T(8,128)S(1)}, f32[32,12288]{1,0:T(8,128)S(1)}, f32[128,12288]{1,0:T(8,128)}, /*index=5*/f32[288,128]{1,0:T(8,128)S(1)}) custom-call(f32[18,96,128]{2,1,0:T(8,128)S(1)} %get-tuple-element.105.geo.refs_0_, f32[8,384]{1,0:T(8,128)S(1)} %get-tuple-element.102.own, ...), custom_call_target="tpu_custom_call" | custom-call | flops 12884901888 | bytes 25165824 | tf_op jit(solution)/shard_map/first_pass/pallas_call | solution.py:392
  29.3 2.0 collective-permute-start.3
  31.3 6.7 %first_pass.3 = (f32[128,12288]{1,0:T(8,128)}, f32[128,12288]{1,0:T(8,128)}, f32[32,12288]{1,0:T(8,128)S(1)}, f32[32,12288]{1,0:T(8,128)S(1)}, f32[128,12288]{1,0:T(8,128)}, /*index=5*/f32[288,256]{1,0:T(8,128)S(1)}) custom-call(f32[18,96,128]{2,1,0:T(8,128)S(1)} %get-tuple-element.105, ...), custom_call_target="tpu_custom_call", output_to_operand_aliasing={{0}: (5, {}), {1}: (6, {}), {2}: (7, {}), {3}: (8, {}), {4}... | custom-call | flops 12884901888 | bytes 25165824 | tf_op jit(solution)/shard_map/first_pass/pallas_call | solution.py:392
  38.7 2.1 collective-permute-start.6
  40.8 12.5 %collective-permute-done.6.refs_5_.refs_13_ = f32[288,256]{1,0:T(8,128)S(1)} collective-permute-done((f32[288,256]{1,0:T(8,128)S(1)}, f32[288,256]{1,0:T(8,128)S(1)}, u32[]{:S(2)}, u32[]{:S(2)}) %collective-permute-start.6) | collective-permute-done | bytes 294944 | tf_op jit(solution)/shard_map/ppermute | solution.py:34
  54.3 1.8 collective-permute-done.7.refs_14_
  56.1 24.5 %middle_pass.2 = (f32[288,12288]{1,0:T(8,128)}, f32[128,12288]{1,0:T(8,128)}, f32[128,12288]{1,0:T(8,128)}, f32[32,12288]{1,0:T(8,128)S(1)}, f32[32,12288]{1,0:T...) custom-call(f32[18,96,128]{2,1,0:T(8,128)S(1)} %get-tuple-element.105.geo.refs_0_, ...), custom_call_target="tpu_custom_call" | custom-call | flops 10871635968 | bytes 21233664 | tf_op jit(solution)/shard_map/middle_pass/pallas_call | solution.py:541
  80.6 3.0 %collective-permute-start.9 = (f32[288,256]{1,0:T(8,128)S(1)}, f32[288,256]{1,0:T(8,128)S(1)}, u32[]{:S(2)}, u32[]{:S(2)}) collective-permute-start(f32[288,256]{1,0:T(8,128)S(1)} %get-tuple-element.136.refs_0_.refs_9_), channel_id=1, source_target_pairs={{0,14},{2,0},{4,2},{6,4},{8,6},{10,8},{12,10},{14,12},{1,15},{3,1}... | collective-permute-start | bytes 884744 | tf_op jit(solution)/shard_map/ppermute | solution.py:34
  83.6 10.2 %collective-permute-start.8 = (f32[288,256]{1,0:T(8,128)S(1)}, f32[288,256]{1,0:T(8,128)S(1)}, u32[]{:S(2)}, u32[]{:S(2)}) collective-permute-start(f32[288,256]{1,0:T(8,128)S(1)} %get-tuple-element.136.refs_0_.refs_9_), channel_id=1, source_target_pairs={{0,2},{2,4},{4,6},{6,8},{8,10},{10,12},{12,14},{14,0},{1,3},{3,5},... | collective-permute-start | bytes 884744 | tf_op jit(solution)/shard_map/ppermute | solution.py:34
  93.9 14.2 %middle_pass.3 = (f32[288,12288]{1,0:T(8,128)}, f32[128,12288]{1,0:T(8,128)}, f32[128,12288]{1,0:T(8,128)}, f32[32,12288]{1,0:T(8,128)S(1)}, f32[32,12288]{1,0:T...) custom-call(f32[18,96,128]{2,1,0:T(8,128)S(1)} %get-tuple-element.10, ...), custom_call_target="tpu_custom_call", output_to_operand_aliasing={{0}: (15, {}), {1}: (16, {}), {2}: (17, {}), {3}: (18, {}),... | custom-call | flops 10871635968 | bytes 21233664 | tf_op jit(solution)/shard_map/middle_pass/pallas_call | solution.py:541
  108.1 4.7 %collective-permute-start.11 = (f32[288,128]{1,0:T(8,128)S(1)}, f32[288,128]{1,0:T(8,128)S(1)}, u32[]{:S(2)}, u32[]{:S(2)}) collective-permute-start(f32[288,128]{1,0:T(8,128)S(1)} %get-tuple-element.139.refs_1_.refs_10_), channel_id=1, source_target_pairs={{0,14},{2,0},{4,2},{6,4},{8,6},{10,8},{12,10},{14,12},{1,15},{3,1}... | collective-permute-start | bytes 442376 | tf_op jit(solution)/shard_map/ppermute | solution.py:34
  112.9 2.8 %collective-permute-done.11.refs_5_.refs_14_ = f32[288,128]{1,0:T(8,128)S(1)} collective-permute-done((f32[288,128]{1,0:T(8,128)S(1)}, f32[288,128]{1,0:T(8,128)S(1)}, u32[]{:S(2)}, u32[]{:S(2)}) %collective-permute-start.11) | collective-permute-done | bytes 147488 | tf_op jit(solution)/shard_map/ppermute | solution.py:34
  115.7 5.0 %collective-permute-done.10.refs_3_.refs_12_ = f32[288,128]{1,0:T(8,128)S(1)} collective-permute-done((f32[288,128]{1,0:T(8,128)S(1)}, f32[288,128]{1,0:T(8,128)S(1)}, u32[]{:S(2)}, u32[]{:S(2)}) %collective-permute-start.10) | collective-permute-done | bytes 147488 | tf_op jit(solution)/shard_map/ppermute | solution.py:34
  121.8 1.8 collective-permute-done.12.refs_15_
  123.5 56.4 %last_pass.1 = (f32[1,384]{1,0:T(1,128)}, f32[8,128]{1,0:T(8,128)S(1)}, f32[128,12288]{1,0:T(8,128)}, f32[32,12288]{1,0:T(8,128)S(1)}, f32[9,96,128]{2,1,0:T(8,1...) custom-call(f32[18,96,128]{2,1,0:T(8,128)S(1)} %get-tuple-element.105.geo.refs_0_, ...), custom_call_target="tpu_custom_call" | custom-call | flops 21743271936 | bytes 42467328 | tf_op jit(solution)/shard_map/last_pass/pallas_call | solution.py:650
  180.2 1.7 collective-permute-done.13.returned
  184.9 7.1 %collective-permute-done.16 = f32[8,128]{1,0:T(8,128)S(1)} collective-permute-done((f32[8,128]{1,0:T(8,128)S(1)}, f32[8,128]{1,0:T(8,128)S(1)}, u32[]{:S(2)}, u32[]{:S(2)}) %collective-permute-start.16) | collective-permute-done | bytes 4128 | tf_op jit(solution)/shard_map/ppermute | solution.py:34
  194.1 13.8 %middle_back.2 = (f32[128,12288]{1,0:T(8,128)}, f32[32,12288]{1,0:T(8,128)S(1)}, f32[9,96,128]{2,1,0:T(8,128)S(1)}, f32[288,1152]{1,0:T(8,128)S(1)}, f32[288,384]{1,0:T(8,128)S(1)}) custom-call(f32[18,96,128]{2,1,0:T(8,128)S(1)} %get-tuple-element.105.geo.refs_0_, s32[96,128]{1,0:T(8,128)S(1)} %get-tuple-element.106.refs_1_.nbrs, ...), custom_call_target="tpu_custom_call" | custom-call | flops 10871635968 | bytes 21233664 | tf_op jit(solution)/shard_map/middle_back/pallas_call | solution.py:750
  207.9 25.6 %middle_back.3 = (f32[128,12288]{1,0:T(8,128)}, f32[32,12288]{1,0:T(8,128)S(1)}, f32[9,96,128]{2,1,0:T(8,128)S(1)}, f32[288,1152]{1,0:T(8,128)S(1)}, f32[288,384]{1,0:T(8,128)S(1)}) custom-call(f32[18,96,128]{2,1,0:T(8,128)S(1)} %get-tuple-element.105.geo.refs_0_, ...), custom_call_target="tpu_custom_call", output_to_operand_aliasing={{0}: (16, {}), {1}: (17, {}), {2}: (18, {})} | custom-call | flops 10871635968 | bytes 21233664 | tf_op jit(solution)/shard_map/middle_back/pallas_call | solution.py:750
  233.6 1.8 collective-permute-done.19.returned
  236.4 3.5 %collective-permute-start.20 = (f32[288,256]{1,0:T(8,128)S(1)}, f32[288,256]{1,0:T(8,128)S(1)}, u32[]{:S(2)}, u32[]{:S(2)}) collective-permute-start(f32[288,256]{1,0:T(8,128)S(1)} %get-tuple-element.179), channel_id=1, source_target_pairs={{0,14},{2,0},{4,2},{6,4},{8,6},{10,8},{12,10},{14,12},{1,15},{3,1}... | collective-permute-start | bytes 884744 | tf_op jit(solution)/shard_map/ppermute | solution.py:34
  239.9 6.7 %collective-permute-done.22 = f32[8,128]{1,0:T(8,128)S(1)} collective-permute-done((f32[8,128]{1,0:T(8,128)S(1)}, f32[8,128]{1,0:T(8,128)S(1)}, u32[]{:S(2)}, u32[]{:S(2)}) %collective-permute-start.22) | collective-permute-done | bytes 4128 | tf_op jit(solution)/shard_map/ppermute | solution.py:34
  246.6 4.5 %collective-permute-done.23 = f32[8,128]{1,0:T(8,128)S(1)} collective-permute-done((f32[8,128]{1,0:T(8,128)S(1)}, f32[8,128]{1,0:T(8,128)S(1)}, u32[]{:S(2)}, u32[]{:S(2)}) %collective-permute-start.23) | collective-permute-done | bytes 4128 | tf_op jit(solution)/shard_map/ppermute | solution.py:34
  251.8 3.8 %collective-permute-start.24 = (f32[288,128]{1,0:T(8,128)S(1)}, f32[288,128]{1,0:T(8,128)S(1)}, u32[]{:S(2)}, u32[]{:S(2)}) collective-permute-start(f32[288,128]{1,0:T(8,128)S(1)} %get-tuple-element.182), channel_id=1, source_target_pairs={{0,14},{2,0},{4,2},{6,4},{8,6},{10,8},{12,10},{14,12},{1,15},{3,1}... | collective-permute-start | bytes 442376 | tf_op jit(solution)/shard_map/ppermute | solution.py:34
  257.0 6.4 %first_back.2.rest_0_ = f32[17,96,128]{2,1,0:T(8,128)S(1)} custom-call(f32[18,96,128]{2,1,0:T(8,128)S(1)} %get-tuple-element.105.geo.refs_0_, f32[288,256]{1,0:T(8,128)S(1)} %get-tuple-element.190.own, f32[288,256]{1,0:T(8,128)S(1)} %collective-permute-done.20.low, f32[288,256]{1,0:T(8,128)S(1)} %collective-permute-done.21.high, ...), custom_call_target="tpu_custom_call" | custom-call | flops 12884901888 | bytes 25165824 | tf_op jit(solution)/shard_map/first_back/pallas_call | solution.py:809
  263.7 3.6 %first_back.3.dgeo = f32[17,96,128]{2,1,0:T(8,128)S(1)} custom-call(f32[18,96,128]{2,1,0:T(8,128)S(1)} %get-tuple-element.105.geo.refs_0_, f32[288,128]{1,0:T(8,128)S(1)} %get-tuple-element.175.own, f32[288,128]{1,0:T(8,128)S(1)} %collective-permute-done.24.low, f32[288,128]{1,0:T(8,128)S(1)} %collective-permute-done.25.high, ...), custom_call_target="tpu_custom_call", output_to_operand_aliasing={{}: (11, {})} | custom-call | flops 12884901888 | bytes 25165824 | tf_op jit(solution)/shard_map/first_back/pallas_call | solution.py:809
  267.3 1.6 geometry_back.1
  270.5 3.4 %collective-permute-start.27 = (f32[8,384]{1,0:T(8,128)S(1)}, f32[8,384]{1,0:T(8,128)S(1)}, u32[]{:S(2)}, u32[]{:S(2)}) collective-permute-start(f32[8,384]{1,0:T(8,128)S(1)} %get-tuple-element.198), channel_id=1, source_target_pairs={{0,14},{2,0},{4,2},{6,4},{8,6},{10,8},{12,10},{14,12},{1,15},{3,1}... | collective-permute-start | bytes 36872 | tf_op jit(solution)/shard_map/ppermute | solution.py:34
  275.3 5.0 %collective-permute-done.28 = f32[8,384]{1,0:T(8,128)S(1)} collective-permute-done((f32[8,384]{1,0:T(8,128)S(1)}, f32[8,384]{1,0:T(8,128)S(1)}, u32[]{:S(2)}, u32[]{:S(2)}) %collective-permute-start.28) | collective-permute-done | bytes 12320 | tf_op jit(solution)/shard_map/ppermute | solution.py:34
  (82 shorter events, 25.9 us)
Async XLA Ops:
  3.4 7.4 %collective-permute-start.1 = (f32[8,384]{1,0:T(8,128)S(1)}, f32[8,384]{1,0:T(8,128)S(1)}, u32[]{:S(2)}, u32[]{:S(2)}) collective-permute-start(f32[8,384]{1,0:T(8,128)S(1)} %get-tuple-element.102.own), channel_id=1, source_target_pairs={{0,14},{2,0},{4,2},{6,4},{8,6},{10,8},{12,10},{14,12},{1,15},{3,1}... | collective-permute-start | bytes 36872 | tf_op jit(solution)/shard_map/ppermute | solution.py:34
  9.4 6.4 %collective-permute-start = (f32[8,384]{1,0:T(8,128)S(1)}, f32[8,384]{1,0:T(8,128)S(1)}, u32[]{:S(2)}, u32[]{:S(2)}) collective-permute-start(f32[8,384]{1,0:T(8,128)S(1)} %get-tuple-element.102.own), channel_id=1, source_target_pairs={{0,2},{2,4},{4,6},{6,8},{8,10},{10,12},{12,14},{14,0},{1,3},{3,5},... | collective-permute-start | bytes 36872 | tf_op jit(solution)/shard_map/ppermute | solution.py:34
  16.0 5.5 %collective-permute-start.2 = (f32[8,384]{1,0:T(8,128)S(1)}, f32[8,384]{1,0:T(8,128)S(1)}, u32[]{:S(2)}, u32[]{:S(2)}) collective-permute-start(f32[8,384]{1,0:T(8,128)S(1)} %get-tuple-element.104), channel_id=1, source_target_pairs={{0,1},{1,0},{2,3},{3,2},{4,5},{5,4},{6,7},{7,6},{8,9},{9,8},{10,11... | collective-permute-start | bytes 36872 | tf_op jit(solution)/shard_map/ppermute | solution.py:34
  29.3 9.4 %collective-permute-start.4 = (f32[288,128]{1,0:T(8,128)S(1)}, f32[288,128]{1,0:T(8,128)S(1)}, u32[]{:S(2)}, u32[]{:S(2)}) collective-permute-start(f32[288,128]{1,0:T(8,128)S(1)} %get-tuple-element.119.refs_0_.refs_8_), channel_id=1, source_target_pairs={{0,14},{2,0},{4,2},{6,4},{8,6},{10,8},{12,10},{14,12},{1,15},{3,1}... | collective-permute-start | bytes 442376 | tf_op jit(solution)/shard_map/ppermute | solution.py:34
  29.3 9.4 %collective-permute-start.3 = (f32[288,128]{1,0:T(8,128)S(1)}, f32[288,128]{1,0:T(8,128)S(1)}, u32[]{:S(2)}, u32[]{:S(2)}) collective-permute-start(f32[288,128]{1,0:T(8,128)S(1)} %get-tuple-element.119.refs_0_.refs_8_), channel_id=1, source_target_pairs={{0,2},{2,4},{4,6},{6,8},{8,10},{10,12},{12,14},{14,0},{1,3},{3,5},... | collective-permute-start | bytes 442376 | tf_op jit(solution)/shard_map/ppermute | solution.py:34
  38.0 55.9 %copy-start.1 = (f32[32,12288]{1,0:T(8,128)}, f32[32,12288]{1,0:T(8,128)S(1)}, u32[]{:S(2)}) copy-start(f32[32,12288]{1,0:T(8,128)S(1)} %get-tuple-element.117.refs_4_.refs_11_) | copy-start | bytes 4718596
  38.7 14.6 %collective-permute-start.6 = (f32[288,256]{1,0:T(8,128)S(1)}, f32[288,256]{1,0:T(8,128)S(1)}, u32[]{:S(2)}, u32[]{:S(2)}) collective-permute-start(f32[288,256]{1,0:T(8,128)S(1)} %get-tuple-element.122.refs_1_.refs_9_), channel_id=1, source_target_pairs={{0,14},{2,0},{4,2},{6,4},{8,6},{10,8},{12,10},{14,12},{1,15},{3,1}... | collective-permute-start | bytes 884744 | tf_op jit(solution)/shard_map/ppermute | solution.py:34
  40.8 12.5 %collective-permute-start.5 = (f32[288,256]{1,0:T(8,128)S(1)}, f32[288,256]{1,0:T(8,128)S(1)}, u32[]{:S(2)}, u32[]{:S(2)}) collective-permute-start(f32[288,256]{1,0:T(8,128)S(1)} %get-tuple-element.122.refs_1_.refs_9_), channel_id=1, source_target_pairs={{0,2},{2,4},{4,6},{6,8},{8,10},{10,12},{12,14},{14,0},{1,3},{3,5},... | collective-permute-start | bytes 884744 | tf_op jit(solution)/shard_map/ppermute | solution.py:34
  54.3 1.9 collective-permute-start.7
  80.6 27.5 %collective-permute-start.9 = (f32[288,256]{1,0:T(8,128)S(1)}, f32[288,256]{1,0:T(8,128)S(1)}, u32[]{:S(2)}, u32[]{:S(2)}) collective-permute-start(f32[288,256]{1,0:T(8,128)S(1)} %get-tuple-element.136.refs_0_.refs_9_), channel_id=1, source_target_pairs={{0,14},{2,0},{4,2},{6,4},{8,6},{10,8},{12,10},{14,12},{1,15},{3,1}... | collective-permute-start | bytes 884744 | tf_op jit(solution)/shard_map/ppermute | solution.py:34
  83.6 24.5 %collective-permute-start.8 = (f32[288,256]{1,0:T(8,128)S(1)}, f32[288,256]{1,0:T(8,128)S(1)}, u32[]{:S(2)}, u32[]{:S(2)}) collective-permute-start(f32[288,256]{1,0:T(8,128)S(1)} %get-tuple-element.136.refs_0_.refs_9_), channel_id=1, source_target_pairs={{0,2},{2,4},{4,6},{6,8},{8,10},{10,12},{12,14},{14,0},{1,3},{3,5},... | collective-permute-start | bytes 884744 | tf_op jit(solution)/shard_map/ppermute | solution.py:34
  108.1 86.0 %copy-start = (f32[32,12288]{1,0:T(8,128)}, f32[32,12288]{1,0:T(8,128)S(1)}, u32[]{:S(2)}) copy-start(f32[32,12288]{1,0:T(8,128)S(1)} %get-tuple-element.159.refs_8_) | copy-start | bytes 4718596
  108.1 7.6 %collective-permute-start.11 = (f32[288,128]{1,0:T(8,128)S(1)}, f32[288,128]{1,0:T(8,128)S(1)}, u32[]{:S(2)}, u32[]{:S(2)}) collective-permute-start(f32[288,128]{1,0:T(8,128)S(1)} %get-tuple-element.139.refs_1_.refs_10_), channel_id=1, source_target_pairs={{0,14},{2,0},{4,2},{6,4},{8,6},{10,8},{12,10},{14,12},{1,15},{3,1}... | collective-permute-start | bytes 442376 | tf_op jit(solution)/shard_map/ppermute | solution.py:34
  112.9 7.8 %collective-permute-start.10 = (f32[288,128]{1,0:T(8,128)S(1)}, f32[288,128]{1,0:T(8,128)S(1)}, u32[]{:S(2)}, u32[]{:S(2)}) collective-permute-start(f32[288,128]{1,0:T(8,128)S(1)} %get-tuple-element.139.refs_1_.refs_10_), channel_id=1, source_target_pairs={{0,2},{2,4},{4,6},{6,8},{8,10},{10,12},{12,14},{14,0},{1,3},{3,5},... | collective-permute-start | bytes 442376 | tf_op jit(solution)/shard_map/ppermute | solution.py:34
  121.7 1.9 collective-permute-start.12
  180.0 1.9 collective-permute-start.13
  182.8 9.2 %collective-permute-start.14 = (f32[288,128]{1,0:T(8,128)S(1)}, f32[288,128]{1,0:T(8,128)S(1)}, u32[]{:S(2)}, u32[]{:S(2)}) collective-permute-start(f32[288,128]{1,0:T(8,128)S(1)} %get-tuple-element.151), channel_id=1, source_target_pairs={{0,14},{2,0},{4,2},{6,4},{8,6},{10,8},{12,10},{14,12},{1,15},{3,1}... | collective-permute-start | bytes 442376 | tf_op jit(solution)/shard_map/ppermute | solution.py:34
  183.6 8.4 %collective-permute-start.15 = (f32[288,128]{1,0:T(8,128)S(1)}, f32[288,128]{1,0:T(8,128)S(1)}, u32[]{:S(2)}, u32[]{:S(2)}) collective-permute-start(f32[288,128]{1,0:T(8,128)S(1)} %get-tuple-element.152), channel_id=1, source_target_pairs={{0,2},{2,4},{4,6},{6,8},{8,10},{10,12},{12,14},{14,0},{1,3},{3,5},... | collective-permute-start | bytes 442376 | tf_op jit(solution)/shard_map/ppermute | solution.py:34
  184.9 7.1 %collective-permute-start.16 = (f32[8,128]{1,0:T(8,128)S(1)}, f32[8,128]{1,0:T(8,128)S(1)}, u32[]{:S(2)}, u32[]{:S(2)}) collective-permute-start(f32[8,128]{1,0:T(8,128)S(1)} %get-tuple-element.153), channel_id=1, source_target_pairs={{0,2},{2,4},{4,6},{6,8},{8,10},{10,12},{12,14},{14,0},{1,3},{3,5},... | collective-permute-start | bytes 12296 | tf_op jit(solution)/shard_map/ppermute | solution.py:34
  192.0 15.9 %collective-permute-start.17 = (f32[288,256]{1,0:T(8,128)S(1)}, f32[288,256]{1,0:T(8,128)S(1)}, u32[]{:S(2)}, u32[]{:S(2)}) collective-permute-start(f32[288,256]{1,0:T(8,128)S(1)} %get-tuple-element.154), channel_id=1, source_target_pairs={{0,14},{2,0},{4,2},{6,4},{8,6},{10,8},{12,10},{14,12},{1,15},{3,1}... | collective-permute-start | bytes 884744 | tf_op jit(solution)/shard_map/ppermute | solution.py:34
  192.9 15.0 %collective-permute-start.18 = (f32[288,256]{1,0:T(8,128)S(1)}, f32[288,256]{1,0:T(8,128)S(1)}, u32[]{:S(2)}, u32[]{:S(2)}) collective-permute-start(f32[288,256]{1,0:T(8,128)S(1)} %get-tuple-element.155), channel_id=1, source_target_pairs={{0,2},{2,4},{4,6},{6,8},{8,10},{10,12},{12,14},{14,0},{1,3},{3,5},... | collective-permute-start | bytes 884744 | tf_op jit(solution)/shard_map/ppermute | solution.py:34
  233.5 1.9 collective-permute-start.19
  236.4 15.4 %collective-permute-start.20 = (f32[288,256]{1,0:T(8,128)S(1)}, f32[288,256]{1,0:T(8,128)S(1)}, u32[]{:S(2)}, u32[]{:S(2)}) collective-permute-start(f32[288,256]{1,0:T(8,128)S(1)} %get-tuple-element.179), channel_id=1, source_target_pairs={{0,14},{2,0},{4,2},{6,4},{8,6},{10,8},{12,10},{14,12},{1,15},{3,1}... | collective-permute-start | bytes 884744 | tf_op jit(solution)/shard_map/ppermute | solution.py:34
  239.9 11.9 %collective-permute-start.21 = (f32[288,256]{1,0:T(8,128)S(1)}, f32[288,256]{1,0:T(8,128)S(1)}, u32[]{:S(2)}, u32[]{:S(2)}) collective-permute-start(f32[288,256]{1,0:T(8,128)S(1)} %get-tuple-element.180), channel_id=1, source_target_pairs={{0,2},{2,4},{4,6},{6,8},{8,10},{10,12},{12,14},{14,0},{1,3},{3,5},... | collective-permute-start | bytes 884744 | tf_op jit(solution)/shard_map/ppermute | solution.py:34
  239.9 6.7 %collective-permute-start.22 = (f32[8,128]{1,0:T(8,128)S(1)}, f32[8,128]{1,0:T(8,128)S(1)}, u32[]{:S(2)}, u32[]{:S(2)}) collective-permute-start(f32[8,128]{1,0:T(8,128)S(1)} %add.18), channel_id=1, source_target_pairs={{0,4},{2,6},{4,8},{6,10},{8,12},{10,14},{12,0},{14,2},{1,5},{3,7},... | collective-permute-start | bytes 12296 | tf_op jit(solution)/shard_map/ppermute | solution.py:34
  246.6 4.5 %collective-permute-start.23 = (f32[8,128]{1,0:T(8,128)S(1)}, f32[8,128]{1,0:T(8,128)S(1)}, u32[]{:S(2)}, u32[]{:S(2)}) collective-permute-start(f32[8,128]{1,0:T(8,128)S(1)} %add.19), channel_id=1, source_target_pairs={{0,8},{2,10},{4,12},{6,14},{8,0},{10,2},{12,4},{14,6},{1,9},{3,11}... | collective-permute-start | bytes 12296 | tf_op jit(solution)/shard_map/ppermute | solution.py:34
  251.8 11.6 %collective-permute-start.24 = (f32[288,128]{1,0:T(8,128)S(1)}, f32[288,128]{1,0:T(8,128)S(1)}, u32[]{:S(2)}, u32[]{:S(2)}) collective-permute-start(f32[288,128]{1,0:T(8,128)S(1)} %get-tuple-element.182), channel_id=1, source_target_pairs={{0,14},{2,0},{4,2},{6,4},{8,6},{10,8},{12,10},{14,12},{1,15},{3,1}... | collective-permute-start | bytes 442376 | tf_op jit(solution)/shard_map/ppermute | solution.py:34
  255.6 8.1 %collective-permute-start.25 = (f32[288,128]{1,0:T(8,128)S(1)}, f32[288,128]{1,0:T(8,128)S(1)}, u32[]{:S(2)}, u32[]{:S(2)}) collective-permute-start(f32[288,128]{1,0:T(8,128)S(1)} %get-tuple-element.183), channel_id=1, source_target_pairs={{0,2},{2,4},{4,6},{6,8},{8,10},{10,12},{12,14},{14,0},{1,3},{3,5},... | collective-permute-start | bytes 442376 | tf_op jit(solution)/shard_map/ppermute | solution.py:34
  268.9 1.2 collective-permute-start.26
  269.0 4.9 %collective-permute-start.29 = (f32[8,128]{1,0:T(8,128)S(1)}, f32[8,128]{1,0:T(8,128)S(1)}, u32[]{:S(2)}, u32[]{:S(2)}) collective-permute-start(f32[8,128]{1,0:T(8,128)S(1)} %add.20), channel_id=1, source_target_pairs={{0,1},{1,0},{2,3},{3,2},{4,5},{5,4},{6,7},{7,6},{8,9},{9,8},{10,11... | collective-permute-start | bytes 12296 | tf_op jit(solution)/shard_map/ppermute | solution.py:34
  270.5 4.8 %collective-permute-start.27 = (f32[8,384]{1,0:T(8,128)S(1)}, f32[8,384]{1,0:T(8,128)S(1)}, u32[]{:S(2)}, u32[]{:S(2)}) collective-permute-start(f32[8,384]{1,0:T(8,128)S(1)} %get-tuple-element.198), channel_id=1, source_target_pairs={{0,14},{2,0},{4,2},{6,4},{8,6},{10,8},{12,10},{14,12},{1,15},{3,1}... | collective-permute-start | bytes 36872 | tf_op jit(solution)/shard_map/ppermute | solution.py:34
  273.9 6.4 %collective-permute-start.28 = (f32[8,384]{1,0:T(8,128)S(1)}, f32[8,384]{1,0:T(8,128)S(1)}, u32[]{:S(2)}, u32[]{:S(2)}) collective-permute-start(f32[8,384]{1,0:T(8,128)S(1)} %get-tuple-element.199), channel_id=1, source_target_pairs={{0,2},{2,4},{4,6},{6,8},{8,10},{10,12},{12,14},{14,0},{1,3},{3,5},... | collective-permute-start | bytes 36872 | tf_op jit(solution)/shard_map/ppermute | solution.py:34
  (12 other events, 8.7 us)

commit v3 on v2

--- a/solution.py
+++ b/solution.py
@@ -25,8 +25,8 @@
 SCALARS = pl.BlockSpec(memory_space=pltpu.SMEM)
 
 
-def params():
-    return pltpu.CompilerParams(vmem_limit_bytes=44 << 20)
+def params(mib=44):
+    return pltpu.CompilerParams(vmem_limit_bytes=mib << 20)
 
 
 def passed_along(value, axis, by):
@@ -131,7 +131,7 @@
         out_shape=out_shape,
         in_specs=[WHOLE] * 7,
         out_specs=[WHOLE] * 7,
-        compiler_params=params(),
+        compiler_params=params(60),
         name="prepare_weights",
     )(two, bias[None], env.swapaxes(1, 2), val.swapaxes(1, 2), lat, lat_bias, out_w[None])
 
@@ -196,7 +196,7 @@
         out_shape=[edge_shape(8, atoms), jax.ShapeDtypeStruct((1, atoms), jnp.int32)],
         in_specs=[WHOLE] * 4,
         out_specs=[WHOLE] * 2,
-        compiler_params=params(),
+        compiler_params=params(60),
         name="pack_rows",
     )(coords, species, lend_x, lend_y)
 

time: 286 us -> 287 us (level)
  Pallas kernels: 164 us -> 167 us
    unnamed x30 -> x32, local copies, waits for them, and re-layouts: 9.93 us -> 8.12 us
where the time goes in v3:
time: 287 us; the launch traced here: 284 us
  Pallas kernels  167 us (58%)
  waiting for transfers between devices  59.7 us (21%)
  starting transfers between devices  45.4 us (16%)
  local copies, waits for them, and re-layouts  8.12 us (3%)
  between operations  3.11 us (1%)
    ppermute x30, waiting for transfers between devices, passed_along(): lax.ppermute(value, axis, [(i, (i + by) % count) for i in range(count)])  59.7 us
    pallas_call x1, Pallas kernels, last_pass(): pl.pallas_call(partial(last_kernel, group=group, per=per, norm=1.0 / math...  56.5 us
    ppermute x30, starting transfers between devices, passed_along(): lax.ppermute(value, axis, [(i, (i + by) % count) for i in range(count)])  45.4 us
    pallas_call x2, Pallas kernels, middle_back(): pl.pallas_call(partial(middle_back_kernel, group=group, per=per, norm=1.0...  39.4 us
    pallas_call x2, Pallas kernels, middle_pass(): pl.pallas_call(partial(middle_kernel, group=group, per=per, norm=1.0 / ma...  38.7 us
    pallas_call x2, Pallas kernels, first_pass(): pl.pallas_call(partial(first_kernel, group=group, per=per, norm=1.0 / mat...  10.6 us
    pallas_call x2, Pallas kernels, first_back(): pl.pallas_call(partial(first_back_kernel, group=group, per=per, norm=1.0...  9.95 us
    unnamed x32, local copies, waits for them, and re-layouts  8.12 us
  transfers between devices with their start and end apart: 30, of which 18 were waited for; matrix products, arithmetic and copies ran while one was open for 0% of the time, Pallas kernels for 15%

profile of v3, /device:TPU:0, one launch (start us, length us, event | category | flops | bytes accessed | tf_op | source)
XLA Modules:
  0.0 284.1 jit_solution(9935822017350318585)
XLA Ops:
  3.3 6.0 %collective-permute-start.1 = (f32[8,384]{1,0:T(8,128)}, f32[8,384]{1,0:T(8,128)S(1)}, u32[]{:S(2)}, u32[]{:S(2)}) collective-permute-start(f32[8,384]{1,0:T(8,128)} %get-tuple-element.102.own), channel_id=1, source_target_pairs={{0,14},{2,0},{4,2},{6,4},{8,6},{10,8},{12,10},{14,12},{1,15},{3,1}... | collective-permute-start | bytes 36872 | tf_op jit(solution)/shard_map/ppermute | solution.py:34
  10.9 5.0 %collective-permute-done.below = f32[8,384]{1,0:T(8,128)S(1)} collective-permute-done((f32[8,384]{1,0:T(8,128)}, f32[8,384]{1,0:T(8,128)S(1)}, u32[]{:S(2)}, u32[]{:S(2)}) %collective-permute-start) | collective-permute-done | bytes 12320 | tf_op jit(solution)/shard_map/ppermute | solution.py:34
  17.5 2.2 prepare_weights.1
  21.9 2.3 geometry.1
  26.8 3.9 %first_pass.2 = (f32[128,12288]{1,0:T(8,128)}, f32[128,12288]{1,0:T(8,128)}, f32[32,12288]{1,0:T(8,128)S(1)}, f32[32,12288]{1,0:T(8,128)S(1)}, f32[128,12288]{1,0:T(8,128)}, /*index=5*/f32[288,128]{1,0:T(8,128)S(1)}) custom-call(f32[18,96,128]{2,1,0:T(8,128)S(1)} %get-tuple-element.105.geo.refs_0_, f32[8,384]{1,0:T(8,128)S(1)} %copy-done.10, ...), custom_call_target="tpu_custom_call" | custom-call | flops 12884901888 | bytes 25165824 | tf_op jit(solution)/shard_map/first_pass/pallas_call | solution.py:392
  30.8 2.0 collective-permute-start.3
  32.8 6.7 %first_pass.3 = (f32[128,12288]{1,0:T(8,128)}, f32[128,12288]{1,0:T(8,128)}, f32[32,12288]{1,0:T(8,128)S(1)}, f32[32,12288]{1,0:T(8,128)S(1)}, f32[128,12288]{1,0:T(8,128)}, /*index=5*/f32[288,256]{1,0:T(8,128)S(1)}) custom-call(f32[18,96,128]{2,1,0:T(8,128)S(1)} %get-tuple-element.105, ...), custom_call_target="tpu_custom_call", output_to_operand_aliasing={{0}: (5, {}), {1}: (6, {}), {2}: (7, {}), {3}: (8, {}), {4}... | custom-call | flops 12884901888 | bytes 25165824 | tf_op jit(solution)/shard_map/first_pass/pallas_call | solution.py:392
  40.2 2.1 collective-permute-start.6
  42.2 12.5 %collective-permute-done.6.refs_5_.refs_13_ = f32[288,256]{1,0:T(8,128)S(1)} collective-permute-done((f32[288,256]{1,0:T(8,128)S(1)}, f32[288,256]{1,0:T(8,128)S(1)}, u32[]{:S(2)}, u32[]{:S(2)}) %collective-permute-start.6) | collective-permute-done | bytes 294944 | tf_op jit(solution)/shard_map/ppermute | solution.py:34
  55.8 1.8 collective-permute-done.7.refs_14_
  57.6 24.4 %middle_pass.2 = (f32[288,12288]{1,0:T(8,128)}, f32[128,12288]{1,0:T(8,128)}, f32[128,12288]{1,0:T(8,128)}, f32[32,12288]{1,0:T(8,128)S(1)}, f32[32,12288]{1,0:T...) custom-call(f32[18,96,128]{2,1,0:T(8,128)S(1)} %get-tuple-element.105.geo.refs_0_, ...), custom_call_target="tpu_custom_call" | custom-call | flops 10871635968 | bytes 21233664 | tf_op jit(solution)/shard_map/middle_pass/pallas_call | solution.py:541
  82.0 3.0 %collective-permute-start.9 = (f32[288,256]{1,0:T(8,128)S(1)}, f32[288,256]{1,0:T(8,128)S(1)}, u32[]{:S(2)}, u32[]{:S(2)}) collective-permute-start(f32[288,256]{1,0:T(8,128)S(1)} %get-tuple-element.136.refs_0_.refs_9_), channel_id=1, source_target_pairs={{0,14},{2,0},{4,2},{6,4},{8,6},{10,8},{12,10},{14,12},{1,15},{3,1}... | collective-permute-start | bytes 884744 | tf_op jit(solution)/shard_map/ppermute | solution.py:34
  85.1 10.2 %collective-permute-start.8 = (f32[288,256]{1,0:T(8,128)S(1)}, f32[288,256]{1,0:T(8,128)S(1)}, u32[]{:S(2)}, u32[]{:S(2)}) collective-permute-start(f32[288,256]{1,0:T(8,128)S(1)} %get-tuple-element.136.refs_0_.refs_9_), channel_id=1, source_target_pairs={{0,2},{2,4},{4,6},{6,8},{8,10},{10,12},{12,14},{14,0},{1,3},{3,5},... | collective-permute-start | bytes 884744 | tf_op jit(solution)/shard_map/ppermute | solution.py:34
  95.3 14.3 %middle_pass.3 = (f32[288,12288]{1,0:T(8,128)}, f32[128,12288]{1,0:T(8,128)}, f32[128,12288]{1,0:T(8,128)}, f32[32,12288]{1,0:T(8,128)S(1)}, f32[32,12288]{1,0:T...) custom-call(f32[18,96,128]{2,1,0:T(8,128)S(1)} %get-tuple-element.10, ...), custom_call_target="tpu_custom_call", output_to_operand_aliasing={{0}: (15, {}), {1}: (16, {}), {2}: (17, {}), {3}: (18, {}),... | custom-call | flops 10871635968 | bytes 21233664 | tf_op jit(solution)/shard_map/middle_pass/pallas_call | solution.py:541
  109.6 4.7 %collective-permute-start.11 = (f32[288,128]{1,0:T(8,128)S(1)}, f32[288,128]{1,0:T(8,128)S(1)}, u32[]{:S(2)}, u32[]{:S(2)}) collective-permute-start(f32[288,128]{1,0:T(8,128)S(1)} %get-tuple-element.139.refs_1_.refs_10_), channel_id=1, source_target_pairs={{0,14},{2,0},{4,2},{6,4},{8,6},{10,8},{12,10},{14,12},{1,15},{3,1}... | collective-permute-start | bytes 442376 | tf_op jit(solution)/shard_map/ppermute | solution.py:34
  114.4 2.8 %collective-permute-done.11.refs_5_.refs_14_ = f32[288,128]{1,0:T(8,128)S(1)} collective-permute-done((f32[288,128]{1,0:T(8,128)S(1)}, f32[288,128]{1,0:T(8,128)S(1)}, u32[]{:S(2)}, u32[]{:S(2)}) %collective-permute-start.11) | collective-permute-done | bytes 147488 | tf_op jit(solution)/shard_map/ppermute | solution.py:34
  117.2 5.0 %collective-permute-done.10.refs_3_.refs_12_ = f32[288,128]{1,0:T(8,128)S(1)} collective-permute-done((f32[288,128]{1,0:T(8,128)S(1)}, f32[288,128]{1,0:T(8,128)S(1)}, u32[]{:S(2)}, u32[]{:S(2)}) %collective-permute-start.10) | collective-permute-done | bytes 147488 | tf_op jit(solution)/shard_map/ppermute | solution.py:34
  123.3 1.8 collective-permute-done.12.refs_15_
  125.0 56.5 %last_pass.1 = (f32[1,384]{1,0:T(1,128)}, f32[8,128]{1,0:T(8,128)S(1)}, f32[128,12288]{1,0:T(8,128)}, f32[32,12288]{1,0:T(8,128)S(1)}, f32[9,96,128]{2,1,0:T(8,1...) custom-call(f32[18,96,128]{2,1,0:T(8,128)S(1)} %get-tuple-element.105.geo.refs_0_, ...), custom_call_target="tpu_custom_call" | custom-call | flops 21743271936 | bytes 42467328 | tf_op jit(solution)/shard_map/last_pass/pallas_call | solution.py:650
  181.7 1.7 collective-permute-done.13.returned
  186.5 7.1 %collective-permute-done.16 = f32[8,128]{1,0:T(8,128)S(1)} collective-permute-done((f32[8,128]{1,0:T(8,128)S(1)}, f32[8,128]{1,0:T(8,128)S(1)}, u32[]{:S(2)}, u32[]{:S(2)}) %collective-permute-start.16) | collective-permute-done | bytes 4128 | tf_op jit(solution)/shard_map/ppermute | solution.py:34
  195.7 13.8 %middle_back.2 = (f32[128,12288]{1,0:T(8,128)}, f32[32,12288]{1,0:T(8,128)S(1)}, f32[9,96,128]{2,1,0:T(8,128)S(1)}, f32[288,1152]{1,0:T(8,128)S(1)}, f32[288,384]{1,0:T(8,128)S(1)}) custom-call(f32[18,96,128]{2,1,0:T(8,128)S(1)} %get-tuple-element.105.geo.refs_0_, s32[96,128]{1,0:T(8,128)S(1)} %get-tuple-element.106.refs_1_.nbrs, ...), custom_call_target="tpu_custom_call" | custom-call | flops 10871635968 | bytes 21233664 | tf_op jit(solution)/shard_map/middle_back/pallas_call | solution.py:750
  209.5 25.6 %middle_back.3 = (f32[128,12288]{1,0:T(8,128)}, f32[32,12288]{1,0:T(8,128)S(1)}, f32[9,96,128]{2,1,0:T(8,128)S(1)}, f32[288,1152]{1,0:T(8,128)S(1)}, f32[288,384]{1,0:T(8,128)S(1)}) custom-call(f32[18,96,128]{2,1,0:T(8,128)S(1)} %get-tuple-element.105.geo.refs_0_, ...), custom_call_target="tpu_custom_call", output_to_operand_aliasing={{0}: (16, {}), {1}: (17, {}), {2}: (18, {})} | custom-call | flops 10871635968 | bytes 21233664 | tf_op jit(solution)/shard_map/middle_back/pallas_call | solution.py:750
  235.2 1.8 collective-permute-done.19.returned
  238.0 3.5 %collective-permute-start.20 = (f32[288,256]{1,0:T(8,128)S(1)}, f32[288,256]{1,0:T(8,128)S(1)}, u32[]{:S(2)}, u32[]{:S(2)}) collective-permute-start(f32[288,256]{1,0:T(8,128)S(1)} %get-tuple-element.179), channel_id=1, source_target_pairs={{0,14},{2,0},{4,2},{6,4},{8,6},{10,8},{12,10},{14,12},{1,15},{3,1}... | collective-permute-start | bytes 884744 | tf_op jit(solution)/shard_map/ppermute | solution.py:34
  241.6 6.7 %collective-permute-done.22 = f32[8,128]{1,0:T(8,128)S(1)} collective-permute-done((f32[8,128]{1,0:T(8,128)S(1)}, f32[8,128]{1,0:T(8,128)S(1)}, u32[]{:S(2)}, u32[]{:S(2)}) %collective-permute-start.22) | collective-permute-done | bytes 4128 | tf_op jit(solution)/shard_map/ppermute | solution.py:34
  248.3 4.5 %collective-permute-done.23 = f32[8,128]{1,0:T(8,128)S(1)} collective-permute-done((f32[8,128]{1,0:T(8,128)S(1)}, f32[8,128]{1,0:T(8,128)S(1)}, u32[]{:S(2)}, u32[]{:S(2)}) %collective-permute-start.23) | collective-permute-done | bytes 4128 | tf_op jit(solution)/shard_map/ppermute | solution.py:34
  253.5 3.8 %collective-permute-start.24 = (f32[288,128]{1,0:T(8,128)S(1)}, f32[288,128]{1,0:T(8,128)S(1)}, u32[]{:S(2)}, u32[]{:S(2)}) collective-permute-start(f32[288,128]{1,0:T(8,128)S(1)} %get-tuple-element.182), channel_id=1, source_target_pairs={{0,14},{2,0},{4,2},{6,4},{8,6},{10,8},{12,10},{14,12},{1,15},{3,1}... | collective-permute-start | bytes 442376 | tf_op jit(solution)/shard_map/ppermute | solution.py:34
  258.6 6.4 %first_back.2.rest_0_ = f32[17,96,128]{2,1,0:T(8,128)S(1)} custom-call(f32[18,96,128]{2,1,0:T(8,128)S(1)} %get-tuple-element.105.geo.refs_0_, f32[288,256]{1,0:T(8,128)S(1)} %get-tuple-element.190.own, f32[288,256]{1,0:T(8,128)S(1)} %collective-permute-done.20.low, f32[288,256]{1,0:T(8,128)S(1)} %collective-permute-done.21.high, ...), custom_call_target="tpu_custom_call" | custom-call | flops 12884901888 | bytes 25165824 | tf_op jit(solution)/shard_map/first_back/pallas_call | solution.py:809
  265.3 3.6 %first_back.3.dgeo = f32[17,96,128]{2,1,0:T(8,128)S(1)} custom-call(f32[18,96,128]{2,1,0:T(8,128)S(1)} %get-tuple-element.105.geo.refs_0_, f32[288,128]{1,0:T(8,128)S(1)} %get-tuple-element.175.own, f32[288,128]{1,0:T(8,128)S(1)} %collective-permute-done.24.low, f32[288,128]{1,0:T(8,128)S(1)} %collective-permute-done.25.high, ...), custom_call_target="tpu_custom_call", output_to_operand_aliasing={{}: (11, {})} | custom-call | flops 12884901888 | bytes 25165824 | tf_op jit(solution)/shard_map/first_back/pallas_call | solution.py:809
  272.2 3.4 %collective-permute-start.27 = (f32[8,384]{1,0:T(8,128)S(1)}, f32[8,384]{1,0:T(8,128)S(1)}, u32[]{:S(2)}, u32[]{:S(2)}) collective-permute-start(f32[8,384]{1,0:T(8,128)S(1)} %get-tuple-element.198), channel_id=1, source_target_pairs={{0,14},{2,0},{4,2},{6,4},{8,6},{10,8},{12,10},{14,12},{1,15},{3,1}... | collective-permute-start | bytes 36872 | tf_op jit(solution)/shard_map/ppermute | solution.py:34
  276.9 5.0 %collective-permute-done.28 = f32[8,384]{1,0:T(8,128)S(1)} collective-permute-done((f32[8,384]{1,0:T(8,128)S(1)}, f32[8,384]{1,0:T(8,128)S(1)}, u32[]{:S(2)}, u32[]{:S(2)}) %collective-permute-start.28) | collective-permute-done | bytes 12320 | tf_op jit(solution)/shard_map/ppermute | solution.py:34
  (84 shorter events, 27.0 us)
Async XLA Ops:
  3.3 7.6 %collective-permute-start.1 = (f32[8,384]{1,0:T(8,128)}, f32[8,384]{1,0:T(8,128)S(1)}, u32[]{:S(2)}, u32[]{:S(2)}) collective-permute-start(f32[8,384]{1,0:T(8,128)} %get-tuple-element.102.own), channel_id=1, source_target_pairs={{0,14},{2,0},{4,2},{6,4},{8,6},{10,8},{12,10},{14,12},{1,15},{3,1}... | collective-permute-start | bytes 36872 | tf_op jit(solution)/shard_map/ppermute | solution.py:34
  9.3 6.6 %collective-permute-start = (f32[8,384]{1,0:T(8,128)}, f32[8,384]{1,0:T(8,128)S(1)}, u32[]{:S(2)}, u32[]{:S(2)}) collective-permute-start(f32[8,384]{1,0:T(8,128)} %get-tuple-element.102.own), channel_id=1, source_target_pairs={{0,2},{2,4},{4,6},{6,8},{8,10},{10,12},{12,14},{14,0},{1,3},{3,5},... | collective-permute-start | bytes 36872 | tf_op jit(solution)/shard_map/ppermute | solution.py:34
  17.5 2.3 collective-permute-start.2
  30.8 9.4 %collective-permute-start.4 = (f32[288,128]{1,0:T(8,128)S(1)}, f32[288,128]{1,0:T(8,128)S(1)}, u32[]{:S(2)}, u32[]{:S(2)}) collective-permute-start(f32[288,128]{1,0:T(8,128)S(1)} %get-tuple-element.119.refs_0_.refs_8_), channel_id=1, source_target_pairs={{0,14},{2,0},{4,2},{6,4},{8,6},{10,8},{12,10},{14,12},{1,15},{3,1}... | collective-permute-start | bytes 442376 | tf_op jit(solution)/shard_map/ppermute | solution.py:34
  30.8 9.4 %collective-permute-start.3 = (f32[288,128]{1,0:T(8,128)S(1)}, f32[288,128]{1,0:T(8,128)S(1)}, u32[]{:S(2)}, u32[]{:S(2)}) collective-permute-start(f32[288,128]{1,0:T(8,128)S(1)} %get-tuple-element.119.refs_0_.refs_8_), channel_id=1, source_target_pairs={{0,2},{2,4},{4,6},{6,8},{8,10},{10,12},{12,14},{14,0},{1,3},{3,5},... | collective-permute-start | bytes 442376 | tf_op jit(solution)/shard_map/ppermute | solution.py:34
  40.2 14.5 %collective-permute-start.6 = (f32[288,256]{1,0:T(8,128)S(1)}, f32[288,256]{1,0:T(8,128)S(1)}, u32[]{:S(2)}, u32[]{:S(2)}) collective-permute-start(f32[288,256]{1,0:T(8,128)S(1)} %get-tuple-element.122.refs_1_.refs_9_), channel_id=1, source_target_pairs={{0,14},{2,0},{4,2},{6,4},{8,6},{10,8},{12,10},{14,12},{1,15},{3,1}... | collective-permute-start | bytes 884744 | tf_op jit(solution)/shard_map/ppermute | solution.py:34
  42.2 12.5 %collective-permute-start.5 = (f32[288,256]{1,0:T(8,128)S(1)}, f32[288,256]{1,0:T(8,128)S(1)}, u32[]{:S(2)}, u32[]{:S(2)}) collective-permute-start(f32[288,256]{1,0:T(8,128)S(1)} %get-tuple-element.122.refs_1_.refs_9_), channel_id=1, source_target_pairs={{0,2},{2,4},{4,6},{6,8},{8,10},{10,12},{12,14},{14,0},{1,3},{3,5},... | collective-permute-start | bytes 884744 | tf_op jit(solution)/shard_map/ppermute | solution.py:34
  55.7 1.9 collective-permute-start.7
  82.0 27.6 %collective-permute-start.9 = (f32[288,256]{1,0:T(8,128)S(1)}, f32[288,256]{1,0:T(8,128)S(1)}, u32[]{:S(2)}, u32[]{:S(2)}) collective-permute-start(f32[288,256]{1,0:T(8,128)S(1)} %get-tuple-element.136.refs_0_.refs_9_), channel_id=1, source_target_pairs={{0,14},{2,0},{4,2},{6,4},{8,6},{10,8},{12,10},{14,12},{1,15},{3,1}... | collective-permute-start | bytes 884744 | tf_op jit(solution)/shard_map/ppermute | solution.py:34
  85.1 24.5 %collective-permute-start.8 = (f32[288,256]{1,0:T(8,128)S(1)}, f32[288,256]{1,0:T(8,128)S(1)}, u32[]{:S(2)}, u32[]{:S(2)}) collective-permute-start(f32[288,256]{1,0:T(8,128)S(1)} %get-tuple-element.136.refs_0_.refs_9_), channel_id=1, source_target_pairs={{0,2},{2,4},{4,6},{6,8},{8,10},{10,12},{12,14},{14,0},{1,3},{3,5},... | collective-permute-start | bytes 884744 | tf_op jit(solution)/shard_map/ppermute | solution.py:34
  109.6 86.1 %copy-start = (f32[32,12288]{1,0:T(8,128)}, f32[32,12288]{1,0:T(8,128)S(1)}, u32[]{:S(2)}) copy-start(f32[32,12288]{1,0:T(8,128)S(1)} %get-tuple-element.159.refs_8_) | copy-start | bytes 4718596
  109.6 7.6 %collective-permute-start.11 = (f32[288,128]{1,0:T(8,128)S(1)}, f32[288,128]{1,0:T(8,128)S(1)}, u32[]{:S(2)}, u32[]{:S(2)}) collective-permute-start(f32[288,128]{1,0:T(8,128)S(1)} %get-tuple-element.139.refs_1_.refs_10_), channel_id=1, source_target_pairs={{0,14},{2,0},{4,2},{6,4},{8,6},{10,8},{12,10},{14,12},{1,15},{3,1}... | collective-permute-start | bytes 442376 | tf_op jit(solution)/shard_map/ppermute | solution.py:34
  114.4 7.8 %collective-permute-start.10 = (f32[288,128]{1,0:T(8,128)S(1)}, f32[288,128]{1,0:T(8,128)S(1)}, u32[]{:S(2)}, u32[]{:S(2)}) collective-permute-start(f32[288,128]{1,0:T(8,128)S(1)} %get-tuple-element.139.refs_1_.refs_10_), channel_id=1, source_target_pairs={{0,2},{2,4},{4,6},{6,8},{8,10},{10,12},{12,14},{14,0},{1,3},{3,5},... | collective-permute-start | bytes 442376 | tf_op jit(solution)/shard_map/ppermute | solution.py:34
  123.2 1.9 collective-permute-start.12
  125.0 70.7 %copy-start.6 = (bf16[2,256,128]{2,1,0:T(8,128)(2,1)S(1)}, bf16[2,256,128]{2,1,0:T(8,128)(2,1)}, u32[]{:S(2)}) copy-start(bf16[2,256,128]{2,1,0:T(8,128)(2,1)} %get-tuple-element.162.refs_12_.ev_w) | copy-start | bytes 393220
  181.5 1.9 collective-permute-start.13
  184.4 9.2 %collective-permute-start.14 = (f32[288,128]{1,0:T(8,128)S(1)}, f32[288,128]{1,0:T(8,128)S(1)}, u32[]{:S(2)}, u32[]{:S(2)}) collective-permute-start(f32[288,128]{1,0:T(8,128)S(1)} %get-tuple-element.151), channel_id=1, source_target_pairs={{0,14},{2,0},{4,2},{6,4},{8,6},{10,8},{12,10},{14,12},{1,15},{3,1}... | collective-permute-start | bytes 442376 | tf_op jit(solution)/shard_map/ppermute | solution.py:34
  185.2 8.4 %collective-permute-start.15 = (f32[288,128]{1,0:T(8,128)S(1)}, f32[288,128]{1,0:T(8,128)S(1)}, u32[]{:S(2)}, u32[]{:S(2)}) collective-permute-start(f32[288,128]{1,0:T(8,128)S(1)} %get-tuple-element.152), channel_id=1, source_target_pairs={{0,2},{2,4},{4,6},{6,8},{8,10},{10,12},{12,14},{14,0},{1,3},{3,5},... | collective-permute-start | bytes 442376 | tf_op jit(solution)/shard_map/ppermute | solution.py:34
  186.5 7.1 %collective-permute-start.16 = (f32[8,128]{1,0:T(8,128)S(1)}, f32[8,128]{1,0:T(8,128)S(1)}, u32[]{:S(2)}, u32[]{:S(2)}) collective-permute-start(f32[8,128]{1,0:T(8,128)S(1)} %get-tuple-element.153), channel_id=1, source_target_pairs={{0,2},{2,4},{4,6},{6,8},{8,10},{10,12},{12,14},{14,0},{1,3},{3,5},... | collective-permute-start | bytes 12296 | tf_op jit(solution)/shard_map/ppermute | solution.py:34
  193.6 15.9 %collective-permute-start.17 = (f32[288,256]{1,0:T(8,128)S(1)}, f32[288,256]{1,0:T(8,128)S(1)}, u32[]{:S(2)}, u32[]{:S(2)}) collective-permute-start(f32[288,256]{1,0:T(8,128)S(1)} %get-tuple-element.154), channel_id=1, source_target_pairs={{0,14},{2,0},{4,2},{6,4},{8,6},{10,8},{12,10},{14,12},{1,15},{3,1}... | collective-permute-start | bytes 884744 | tf_op jit(solution)/shard_map/ppermute | solution.py:34
  194.5 15.1 %collective-permute-start.18 = (f32[288,256]{1,0:T(8,128)S(1)}, f32[288,256]{1,0:T(8,128)S(1)}, u32[]{:S(2)}, u32[]{:S(2)}) collective-permute-start(f32[288,256]{1,0:T(8,128)S(1)} %get-tuple-element.155), channel_id=1, source_target_pairs={{0,2},{2,4},{4,6},{6,8},{8,10},{10,12},{12,14},{14,0},{1,3},{3,5},... | collective-permute-start | bytes 884744 | tf_op jit(solution)/shard_map/ppermute | solution.py:34
  235.2 1.9 collective-permute-start.19
  238.0 15.4 %collective-permute-start.20 = (f32[288,256]{1,0:T(8,128)S(1)}, f32[288,256]{1,0:T(8,128)S(1)}, u32[]{:S(2)}, u32[]{:S(2)}) collective-permute-start(f32[288,256]{1,0:T(8,128)S(1)} %get-tuple-element.179), channel_id=1, source_target_pairs={{0,14},{2,0},{4,2},{6,4},{8,6},{10,8},{12,10},{14,12},{1,15},{3,1}... | collective-permute-start | bytes 884744 | tf_op jit(solution)/shard_map/ppermute | solution.py:34
  241.6 11.9 %collective-permute-start.21 = (f32[288,256]{1,0:T(8,128)S(1)}, f32[288,256]{1,0:T(8,128)S(1)}, u32[]{:S(2)}, u32[]{:S(2)}) collective-permute-start(f32[288,256]{1,0:T(8,128)S(1)} %get-tuple-element.180), channel_id=1, source_target_pairs={{0,2},{2,4},{4,6},{6,8},{8,10},{10,12},{12,14},{14,0},{1,3},{3,5},... | collective-permute-start | bytes 884744 | tf_op jit(solution)/shard_map/ppermute | solution.py:34
  241.6 6.7 %collective-permute-start.22 = (f32[8,128]{1,0:T(8,128)S(1)}, f32[8,128]{1,0:T(8,128)S(1)}, u32[]{:S(2)}, u32[]{:S(2)}) collective-permute-start(f32[8,128]{1,0:T(8,128)S(1)} %add.18), channel_id=1, source_target_pairs={{0,4},{2,6},{4,8},{6,10},{8,12},{10,14},{12,0},{14,2},{1,5},{3,7},... | collective-permute-start | bytes 12296 | tf_op jit(solution)/shard_map/ppermute | solution.py:34
  248.3 4.5 %collective-permute-start.23 = (f32[8,128]{1,0:T(8,128)S(1)}, f32[8,128]{1,0:T(8,128)S(1)}, u32[]{:S(2)}, u32[]{:S(2)}) collective-permute-start(f32[8,128]{1,0:T(8,128)S(1)} %add.19), channel_id=1, source_target_pairs={{0,8},{2,10},{4,12},{6,14},{8,0},{10,2},{12,4},{14,6},{1,9},{3,11}... | collective-permute-start | bytes 12296 | tf_op jit(solution)/shard_map/ppermute | solution.py:34
  253.5 11.6 %collective-permute-start.24 = (f32[288,128]{1,0:T(8,128)S(1)}, f32[288,128]{1,0:T(8,128)S(1)}, u32[]{:S(2)}, u32[]{:S(2)}) collective-permute-start(f32[288,128]{1,0:T(8,128)S(1)} %get-tuple-element.182), channel_id=1, source_target_pairs={{0,14},{2,0},{4,2},{6,4},{8,6},{10,8},{12,10},{14,12},{1,15},{3,1}... | collective-permute-start | bytes 442376 | tf_op jit(solution)/shard_map/ppermute | solution.py:34
  257.3 8.1 %collective-permute-start.25 = (f32[288,128]{1,0:T(8,128)S(1)}, f32[288,128]{1,0:T(8,128)S(1)}, u32[]{:S(2)}, u32[]{:S(2)}) collective-permute-start(f32[288,128]{1,0:T(8,128)S(1)} %get-tuple-element.183), channel_id=1, source_target_pairs={{0,2},{2,4},{4,6},{6,8},{8,10},{10,12},{12,14},{14,0},{1,3},{3,5},... | collective-permute-start | bytes 442376 | tf_op jit(solution)/shard_map/ppermute | solution.py:34
  270.6 1.2 collective-permute-start.26
  270.6 4.9 %collective-permute-start.29 = (f32[8,128]{1,0:T(8,128)S(1)}, f32[8,128]{1,0:T(8,128)S(1)}, u32[]{:S(2)}, u32[]{:S(2)}) collective-permute-start(f32[8,128]{1,0:T(8,128)S(1)} %add.20), channel_id=1, source_target_pairs={{0,1},{1,0},{2,3},{3,2},{4,5},{5,4},{6,7},{7,6},{8,9},{9,8},{10,11... | collective-permute-start | bytes 12296 | tf_op jit(solution)/shard_map/ppermute | solution.py:34
  272.2 4.8 %collective-permute-start.27 = (f32[8,384]{1,0:T(8,128)S(1)}, f32[8,384]{1,0:T(8,128)S(1)}, u32[]{:S(2)}, u32[]{:S(2)}) collective-permute-start(f32[8,384]{1,0:T(8,128)S(1)} %get-tuple-element.198), channel_id=1, source_target_pairs={{0,14},{2,0},{4,2},{6,4},{8,6},{10,8},{12,10},{14,12},{1,15},{3,1}... | collective-permute-start | bytes 36872 | tf_op jit(solution)/shard_map/ppermute | solution.py:34
  275.5 6.4 %collective-permute-start.28 = (f32[8,384]{1,0:T(8,128)S(1)}, f32[8,384]{1,0:T(8,128)S(1)}, u32[]{:S(2)}, u32[]{:S(2)}) collective-permute-start(f32[8,384]{1,0:T(8,128)S(1)} %get-tuple-element.199), channel_id=1, source_target_pairs={{0,2},{2,4},{4,6},{6,8},{8,10},{10,12},{12,14},{14,0},{1,3},{3,5},... | collective-permute-start | bytes 36872 | tf_op jit(solution)/shard_map/ppermute | solution.py:34
  (13 other events, 190.5 us)
